TPU v7x, 1024 devices: a whole 4x4x32 slice. The times are simulated.
1024 devices in a mesh: lon: 32 (over z_lo, core), lat: 32 (over y, z_hi, x).
Axes of the slice: x: 4, y: 4, z: 32 (z_hi: 2, z_lo: 16; z = z_hi * 16 + z_lo), core: 2. Of those that a mesh axis runs over, the one named last changes fastest.
Arguments:
- tracer: float32 [8, 768, 7200], P(None, 'lat', 'lon'), may hold values from -6 to 6
- zonal_wind: float32 [8, 768, 7200], P(None, 'lat', 'lon'), may hold values from -6 to 6
- meridional_wind: float32 [8, 768, 7200], P(None, 'lat', 'lon'), may hold values from -6 to 6
- polar_target: int32 [256], replicated, may hold values from 0 to 255, as said below
- cutoff_wave: int32 [256], replicated, may hold values from 1 to 3599
Outputs:
- tracer_next: float32 [8, 768, 7200], P(None, 'lat', 'lon')
- polar_slots: float32 [256, 8, 7200], P('lat', None, 'lon')
Inputs may be any that keep to these rules, and one draw needn't show every extreme that they name: `polar_target`: each of the 256 slots is named by exactly one polar row, so each lat index owns 8 slots (slot s belongs to lat index s // 8); the polar rows held by one lat index name slots of any one lat index at most 1 times, and that many somewhere.
All inputs are finite; a program needn't handle non-finite values.
Results may differ from a plain program's by a relative error of at most 0.00008.
Values sent between devices are 32-bit elements; how exact they have to be, the bound alone decides.
A program may use at most 32 MiB of HBM per device.

v0:
```python
import math

import jax
import jax.numpy as jnp
from jax import lax
from jax.sharding import PartitionSpec as P

courant_number = 0.4


def extended(array, sides, width, wrap):
    for axis, dim in sides:
        devices, length = (lax.axis_size(axis), array.shape[dim])
        up = [(i, (i + 1) % devices) for i in range(devices if wrap else devices - 1)]
        down = [(j, i) for i, j in up]
        last = lax.slice_in_dim(array, length - width, length, axis=dim)
        initial = lax.slice_in_dim(array, 0, width, axis=dim)
        before = lax.ppermute(last, axis, up)
        after = lax.ppermute(initial, axis, down)
        array = jnp.concatenate([before, array, after], axis=dim)
    return array


def exact_dot(left_side, right_side):
    return jnp.dot(
        left_side, right_side, precision=lax.Precision.HIGHEST, preferred_element_type=jnp.float32
    )


def dot_rows(left_side, right_side):
    return lax.dot_general(
        left_side,
        right_side,
        (((1,), (1,)), ((), ())),
        precision=lax.Precision.HIGHEST,
        preferred_element_type=jnp.float32,
    )


def spectral_tables(offset, block_width, total_lon, wave_count):
    positions = offset + jnp.arange(block_width, dtype=jnp.int32)
    wavenumbers = jnp.arange(wave_count, dtype=jnp.int32)
    phase_turns = positions[:, None] * wavenumbers[None, :] % total_lon
    phase_angle = phase_turns.astype(jnp.float32) * (2.0 * math.pi / total_lon)
    valid_wave = (wavenumbers <= total_lon // 2)[None, :]
    return (
        jnp.where(valid_wave, jnp.cos(phase_angle), 0.0),
        jnp.where(valid_wave, jnp.sin(phase_angle), 0.0),
    )


def wave_weights(cut_rows, total_lon, wave_count):
    wavenumbers = jnp.arange(wave_count, dtype=jnp.int32)
    double = jnp.where((wavenumbers == 0) | (2 * wavenumbers == total_lon), 1.0, 2.0)
    kept_mask = (wavenumbers[None, :] <= cut_rows[:, None]) & (
        wavenumbers[None, :] <= total_lon // 2
    )
    return jnp.where(kept_mask, double[None, :] / total_lon, 0.0)


def shards(tracer, zonal_wind, meridional_wind, polar_target, cutoff_wave):
    levels, lat_dev, lon_dev = tracer.shape
    lat_count = lax.axis_size("lat")
    lon_count = lax.axis_size("lon")
    own_lat = lax.axis_index("lat")
    own_lon = lax.axis_index("lon")
    total_lat = lat_dev * lat_count
    total_lon = lon_dev * lon_count
    half_rows = total_lat // 6
    polar_count = 2 * half_rows
    slots_dev = polar_count // lat_count
    capacity = (min(lat_dev, half_rows) + lat_count - 1) // lat_count
    positions_all = lat_count * capacity
    zonal_pad = extended(jnp.stack([tracer, zonal_wind]), (("lon", 3),), 1, True)
    tracer_zonal = zonal_pad[0]
    wind_zonal = zonal_pad[1]
    east_flux = (
        wind_zonal[:, :, : lon_dev + 1]
        * (tracer_zonal[:, :, : lon_dev + 1] + tracer_zonal[:, :, 1:])
        * 0.5
    )
    zonal_div = east_flux[:, :, 1:] - east_flux[:, :, :-1]
    merid_pad = extended(jnp.stack([tracer, meridional_wind]), (("lat", 2),), 1, False)
    tracer_merid = merid_pad[0]
    wind_merid = merid_pad[1]
    face_rows = own_lat * lat_dev - 1 + jnp.arange(lat_dev + 1, dtype=jnp.int32)
    inside_mask = (face_rows >= 0) & (face_rows < total_lat - 1)
    face_cos = jnp.where(
        inside_mask, jnp.sin((face_rows.astype(jnp.float32) + 1.0) * (math.pi / total_lat)), 0.0
    )
    centre_rows = own_lat * lat_dev + jnp.arange(lat_dev, dtype=jnp.int32)
    centre_cos = jnp.sin((centre_rows.astype(jnp.float32) + 0.5) * (math.pi / total_lat))
    north_flux = (
        wind_merid[:, : lat_dev + 1]
        * face_cos[None, :, None]
        * (tracer_merid[:, : lat_dev + 1] + tracer_merid[:, 1:])
        * 0.5
    )
    merid_div = (north_flux[:, 1:] - north_flux[:, :-1]) / centre_cos[None, :, None]
    increment = -courant_number * (zonal_div + merid_div)
    polar_index = jnp.arange(polar_count, dtype=jnp.int32)
    global_rows = jnp.where(
        polar_index < half_rows, polar_index, polar_index + total_lat - 2 * half_rows
    )
    home_device = global_rows // lat_dev
    dest_device = polar_target // slots_dev
    dest_slot = polar_target % slots_dev
    same_route = (
        (home_device[:, None] == home_device[None, :])
        & (dest_device[:, None] == dest_device[None, :])
        & (polar_index[None, :] < polar_index[:, None])
    )
    arrival_rank = jnp.sum(same_route.astype(jnp.int32), axis=1)
    send_position = dest_device * capacity + arrival_rank
    receive_position = home_device * capacity + arrival_rank
    position_index = jnp.arange(positions_all, dtype=jnp.int32)
    out_pick = (position_index[:, None] == send_position[None, :]) & (home_device == own_lat)[
        None, :
    ]
    local_of = (
        global_rows[:, None] == (own_lat * lat_dev + jnp.arange(lat_dev, dtype=jnp.int32))[None, :]
    )
    send_select = exact_dot(out_pick.astype(jnp.float32), local_of.astype(jnp.float32))
    in_pick = (dest_slot[None, :] == jnp.arange(slots_dev, dtype=jnp.int32)[:, None]) & (
        dest_device == own_lat
    )[None, :]
    receive_onehot = (receive_position[:, None] == position_index[None, :]).astype(jnp.float32)
    receive_select = exact_dot(in_pick.astype(jnp.float32), receive_onehot)
    slot_cut = jnp.sum(jnp.where(in_pick, cutoff_wave[None, :], 0), axis=1)
    outgoing = jnp.einsum("pj,ljx->plx", send_select, increment, precision=lax.Precision.HIGHEST)
    arrived = lax.all_to_all(
        outgoing.reshape(lat_count, capacity, levels, lon_dev),
        "lat",
        split_axis=0,
        concat_axis=0,
        tiled=True,
    )
    slot_rows = jnp.einsum(
        "sp,plx->slx",
        receive_select,
        arrived.reshape(positions_all, levels, lon_dev),
        precision=lax.Precision.HIGHEST,
    )
    flat_count = slots_dev * levels
    flat_rows = slot_rows.reshape(flat_count, lon_dev)
    cut_rows = jnp.repeat(slot_cut, levels)
    padded_waves = (total_lon // 2 + lon_count) // lon_count * lon_count
    share_waves = padded_waves // lon_count
    cosine_table, sine_table = spectral_tables(own_lon * lon_dev, lon_dev, total_lon, padded_waves)
    part_cos = exact_dot(flat_rows, cosine_table)
    part_sin = exact_dot(flat_rows, sine_table)
    share_cos, share_sin = (
        lax.psum_scatter(part_cos, "lon", scatter_dimension=1, tiled=True),
        lax.psum_scatter(part_sin, "lon", scatter_dimension=1, tiled=True),
    )
    weights = wave_weights(cut_rows, total_lon, padded_waves)
    share_weights = lax.dynamic_slice_in_dim(weights, own_lon * share_waves, share_waves, 1)
    whole_cos, whole_sin = (
        lax.all_gather(share_cos * share_weights, "lon", axis=1, tiled=True),
        lax.all_gather(share_sin * share_weights, "lon", axis=1, tiled=True),
    )
    filtered_flat = dot_rows(whole_cos, cosine_table) + dot_rows(whole_sin, sine_table)
    filtered = filtered_flat.reshape(slots_dev, levels, lon_dev)
    back_send = jnp.einsum("sp,slx->plx", receive_select, filtered, precision=lax.Precision.HIGHEST)
    returned = lax.all_to_all(
        back_send.reshape(lat_count, capacity, levels, lon_dev),
        "lat",
        split_axis=0,
        concat_axis=0,
        tiled=True,
    )
    polar_increment = jnp.einsum(
        "pj,plx->ljx",
        send_select,
        returned.reshape(positions_all, levels, lon_dev),
        precision=lax.Precision.HIGHEST,
    )
    polar_local = jnp.sum(local_of.astype(jnp.int32), axis=0) > 0
    tracer_next = tracer + jnp.where(polar_local[None, :, None], polar_increment, increment)
    return (tracer_next, filtered)


def solution(mesh):
    placed = (P(None, "lat", "lon"), P(None, "lat", "lon"), P(None, "lat", "lon"), P(), P())
    return jax.shard_map(
        shards,
        mesh=mesh,
        in_specs=placed,
        out_specs=(P(None, "lat", "lon"), P("lat", None, "lon")),
        check_vma=False,
    )
```

profile of v0, /device:TPU:1, one launch (start us, length us, event | category | flops | bytes accessed | tf_op | source)
XLA Modules:
  0.0 1102.9 jit_solution(8967379795291076775)
XLA Ops:
  7.2 1.0 fusion.64
  8.2 3.9 collective-permute-start.2
  12.2 1.3 collective-permute-start.3
  13.5 1.2 fusion.45
  14.6 4.4 collective-permute-start
  19.0 10.9 collective-permute-start.1
  31.5 0.7 copy-done.2
  33.0 0.9 copy.20
  33.9 46.8 %all-to-all-start = ((f32[32,1,8,225]{3,2,1,0:T(8,128)}), f32[32,1,8,225]{3,2,1,0:T(8,128)S(1)}, u32[]{:S(2)}, u32[]{:S(2)}) async-start(f32[32,1,8,225]{3,2,1,0:T(8,128)} %copy.20), calls=%async_computation | async-start | bytes 524288 | tf_op jit(solution)/shard_map/all_to_all | solution.py:131
  81.1 27.0 %all-to-all-done = f32[32,1,8,225]{3,2,1,0:T(8,128)S(1)} async-done(((f32[32,1,8,225]{3,2,1,0:T(8,128)}), f32[32,1,8,225]{3,2,1,0:T(8,128)S(1)}, u32[]{:S(2)}, u32[]{:S(2)}) %all-to-all-start) | async-done | bytes 230432 | tf_op jit(solution)/shard_map/all_to_all | solution.py:131
  108.4 16.6 %fusion.8 = f32[64,3616]{1,0:T(8,128)} fusion(s32[225]{0:T(256)S(1)} %iota_add_fusion, pred[3616]{0:T(1024)(128)(4,1)S(1)} %iota_compare_fusion.5, f32[8,8,225]{2,0,1:T(8,128)S(1)} %fusion.40), kind=kOutput, calls=%fused_computation.12 | convolution fusion | flops 632980800 | bytes 987812 | tf_op jit(solution)/shard_map/dot_general | solution.py:25
  125.0 16.7 %fusion.6 = f32[64,3616]{1,0:T(8,128)} fusion(s32[225]{0:T(256)S(1)} %iota_add_fusion, pred[3616]{0:T(1024)(128)(4,1)S(1)} %iota_compare_fusion.5, f32[8,8,225]{2,0,1:T(8,128)S(1)} %fusion.40), kind=kOutput, calls=%fused_computation.10 | convolution fusion | flops 632980800 | bytes 987812 | tf_op jit(solution)/shard_map/dot_general | solution.py:25
  142.9 1.3 dynamic-slice
  144.8 671.6 %all-reduce.5.cloned.1.call-done = (f32[64,3616]{1,0:T(8,128)}, f32[64,3616]{1,0:T(8,128)}) async-done(((f32[64,3616]{1,0:T(8,128)}, f32[64,3616]{1,0:T(8,128)}), (f32[64,3616]{1,0:T(8,128)}, f32[64,3616]{1,0:T(8,128)})) %all-reduce.5.cloned.1.call-update) | async-done | bytes 1851408
  816.4 1.0 fusion.57
  817.4 101.0 %all-gather.1 = f32[32,113,64]{1,2,0:T(8,128)S(1)} all-gather(f32[1,113,64]{1,2,0:T(8,128)S(1)} %get-tuple-element.14), channel_id=1, replica_groups=mesh['lon'=32,'lat'=32] {'lon'}, dimensions={0}, use_global_device_ids=true | all-gather | bytes 954624 | tf_op jit(solution)/shard_map/all_gather | solution.py:160
  919.0 0.6 reshape.128
  919.7 92.5 %all-gather = f32[32,113,64]{1,2,0:T(8,128)S(1)} all-gather(f32[1,113,64]{1,2,0:T(8,128)S(1)} %get-tuple-element.15), channel_id=1, replica_groups=mesh['lon'=32,'lat'=32] {'lon'}, dimensions={0}, use_global_device_ids=true | all-gather | bytes 954624 | tf_op jit(solution)/shard_map/all_gather | solution.py:159
  1013.5 16.2 %fusion.5 = f32[64,225]{1,0:T(8,128)S(1)} fusion(f32[3616,64]{0,1:T(8,128)S(1)} %reshape.126, s32[225]{0:T(256)S(1)} %iota_add_fusion, pred[3616]{0:T(1024)(128)(4,1)S(1)} %iota_compare_fusion.5), kind=kOutput, calls=%fused_computation.9 | convolution fusion | flops 632980800 | bytes 987812 | tf_op jit(solution)/shard_map/dot_general | solution.py:31
  1029.7 16.4 %fusion.36 = f32[8,8,225]{2,1,0:T(8,128)S(1)} fusion(f32[64,225]{1,0:T(8,128)S(1)} %fusion.5, f32[3616,64]{0,1:T(8,128)S(1)} %reshape.128, s32[225]{0:T(256)S(1)} %iota_add_fusion, pred[3616]{0:T(1024)(128)(4,1)S(1)} %iota_compare_fusion.5), kind=kOutput, calls=%fused_computation.39 | convolution fusion | flops 632995200 | bytes 1045412 | tf_op jit(solution)/shard_map/dot_general | solution.py:31
  1046.5 0.9 copy.26
  1047.3 20.8 %all-to-all-start.1 = ((f32[32,1,8,225]{3,2,1,0:T(8,128)}), f32[32,1,8,225]{3,2,1,0:T(8,128)S(1)}, u32[]{:S(2)}, u32[]{:S(2)}) async-start(f32[32,1,8,225]{3,2,1,0:T(8,128)} %copy.26), calls=%async_computation.1 | async-start | bytes 524288 | tf_op jit(solution)/shard_map/all_to_all | solution.py:165
  1068.3 26.2 %all-to-all-done.1 = f32[32,1,8,225]{3,2,1,0:T(8,128)S(1)} async-done(((f32[32,1,8,225]{3,2,1,0:T(8,128)}), f32[32,1,8,225]{3,2,1,0:T(8,128)S(1)}, u32[]{:S(2)}, u32[]{:S(2)}) %all-to-all-start.1) | async-done | bytes 230432 | tf_op jit(solution)/shard_map/all_to_all | solution.py:165
  1094.5 1.1 fusion.34
  (51 shorter events, 6.5 us)
Async XLA Ops:
  7.2 23.9 %copy-start = (f32[8,24,225]{2,1,0:T(8,128)S(1)}, f32[8,24,225]{2,1,0:T(8,128)}, u32[]{:S(2)}) copy-start(f32[8,24,225]{2,1,0:T(8,128)} %param.5) | copy-start | bytes 518404
  7.2 23.9 %copy-start.1 = (f32[8,24,225]{2,1,0:T(8,128)S(1)}, f32[8,24,225]{2,1,0:T(8,128)}, u32[]{:S(2)}) copy-start(f32[8,24,225]{2,1,0:T(8,128)} %param.6) | copy-start | bytes 518404
  7.2 22.9 %copy-start.4 = (s32[256]{0:T(256)S(1)}, s32[256]{0:T(256)}, u32[]{:S(2)}) copy-start(s32[256]{0:T(256)} %param.8) | copy-start | bytes 3076
  8.2 23.2 %collective-permute-start.2 = (f32[2,8,1,225]{3,2,1,0:T(1,128)S(1)}, f32[2,8,1,225]{3,2,1,0:T(1,128)S(1)}, u32[]{:S(2)}, u32[]{:S(2)}) collective-permute-start(f32[2,8,1,225]{3,2,1,0:T(1,128)S(1)} %get-tuple-element.12), channel_id=1, source_target_pairs={{0,1},{1,2},{2,3},{3,4},{4,5},{5,6},{6,7},{7,8},{8,9},{9,10},{10,1... | collective-permute-start | bytes 43208 | tf_op jit(solution)/shard_map/ppermute | solution.py:18
  12.2 19.3 %collective-permute-start.3 = (f32[2,8,1,225]{3,2,1,0:T(1,128)S(1)}, f32[2,8,1,225]{3,2,1,0:T(1,128)S(1)}, u32[]{:S(2)}, u32[]{:S(2)}) collective-permute-start(f32[2,8,1,225]{3,2,1,0:T(1,128)S(1)} %get-tuple-element.13), channel_id=1, source_target_pairs={{1,0},{2,1},{3,2},{4,3},{5,4},{6,5},{7,6},{8,7},{9,8},{10,9},{11,1... | collective-permute-start | bytes 43208 | tf_op jit(solution)/shard_map/ppermute | solution.py:19
  14.6 15.9 %collective-permute-start = (f32[2,8,24,1]{3,2,1,0:T(8,128)S(1)}, f32[2,8,24,1]{3,2,1,0:T(8,128)S(1)}, u32[]{:S(2)}, u32[]{:S(2)}) collective-permute-start(f32[2,8,24,1]{3,2,1,0:T(8,128)S(1)} %get-tuple-element.10), channel_id=1, source_target_pairs={{0,32},{32,64},{64,96},{96,128},{128,160},{160,192},{192,224},{224... | collective-permute-start | bytes 4616 | tf_op jit(solution)/shard_map/ppermute | solution.py:18
  19.0 12.0 %collective-permute-start.1 = (f32[2,8,24,1]{3,2,1,0:T(8,128)S(1)}, f32[2,8,24,1]{3,2,1,0:T(8,128)S(1)}, u32[]{:S(2)}, u32[]{:S(2)}) collective-permute-start(f32[2,8,24,1]{3,2,1,0:T(8,128)S(1)} %get-tuple-element.11), channel_id=1, source_target_pairs={{32,0},{64,32},{96,64},{128,96},{160,128},{192,160},{224,192},{256... | collective-permute-start | bytes 4616 | tf_op jit(solution)/shard_map/ppermute | solution.py:19
  31.3 0.9 copy-start.2
  33.9 74.2 %all-to-all-start = ((f32[32,1,8,225]{3,2,1,0:T(8,128)}), f32[32,1,8,225]{3,2,1,0:T(8,128)S(1)}, u32[]{:S(2)}, u32[]{:S(2)}) async-start(f32[32,1,8,225]{3,2,1,0:T(8,128)} %copy.20), calls=%async_computation | async-start | bytes 524288 | tf_op jit(solution)/shard_map/all_to_all | solution.py:131
  80.6 735.8 %all-reduce.5.cloned.1.call-start = ((), (), s32[]{:S(2)}) async-start(), calls=%async_computation.2 | async-start | bytes 3801088
  141.7 0.7 copy-start.5
  1046.0 49.5 %copy-start.3 = (f32[8,8,225]{2,1,0:T(8,128)}, f32[8,8,225]{2,1,0:T(8,128)S(1)}, u32[]{:S(2)}) copy-start(f32[8,8,225]{2,1,0:T(8,128)S(1)} %fusion.36) | copy-start | bytes 172804
  1047.3 47.2 %all-to-all-start.1 = ((f32[32,1,8,225]{3,2,1,0:T(8,128)}), f32[32,1,8,225]{3,2,1,0:T(8,128)S(1)}, u32[]{:S(2)}, u32[]{:S(2)}) async-start(f32[32,1,8,225]{3,2,1,0:T(8,128)} %copy.26), calls=%async_computation.1 | async-start | bytes 524288 | tf_op jit(solution)/shard_map/all_to_all | solution.py:165
Sparse Core Ops, SparseCore 0:
  141.9 674.4 all-reduce.4
where the time goes:
time: 1110 us; the launch traced here: 1100 us
  waiting for transfers between devices  725 us (65%)
  blocking collectives  194 us (17%)
  starting transfers between devices  88.3 us (8%)
  matrix products  68.5 us (6%)
  between operations  15.4 us (1%)
    unnamed x2, waiting for transfers between devices  672 us
    all_gather x1, blocking collectives, shards(): lax.all_gather(share_sin * share_weights, 'lon', axis=1, tiled=True)  101 us
    all_gather x1, blocking collectives, shards(): lax.all_gather(share_cos * share_weights, 'lon', axis=1, tiled=True)  92.5 us
    all_to_all x1, starting transfers between devices, shards(): lax.all_to_all(outgoing.reshape(lat_count, capacity, levels, lon_dev), 'l...  46.8 us
    dot_general x4, matrix products, exact_dot(): jnp.dot(left_side, right_side, precision=lax.Precision.HIGHEST, preferred...  33.8 us
    dot_general x2, matrix products, dot_rows(): lax.dot_general(left_side, right_side, (((1,), (1,)), ((), ())), precisio...  32.6 us
    all_to_all x1, waiting for transfers between devices, shards(): lax.all_to_all(outgoing.reshape(lat_count, capacity, levels, lon_dev), 'l...  27 us
    all_to_all x1, waiting for transfers between devices, shards(): lax.all_to_all(back_send.reshape(lat_count, capacity, levels, lon_dev), '...  26.2 us
  transfers between devices with their start and end apart: 7, of which 4 were waited for; matrix products, arithmetic and copies ran while one was open for 0% of the time, Pallas kernels for 0%

commit v1 on v0

--- a/solution.py
+++ b/solution.py
@@ -2,7 +2,10 @@
 
 import jax
 import jax.numpy as jnp
+import numpy as np
 from jax import lax
+from jax.experimental import pallas as pl
+from jax.experimental.pallas import tpu as pltpu
 from jax.sharding import PartitionSpec as P
 
 courant_number = 0.4
@@ -37,25 +40,90 @@
     )
 
 
-def spectral_tables(offset, block_width, total_lon, wave_count):
-    positions = offset + jnp.arange(block_width, dtype=jnp.int32)
-    wavenumbers = jnp.arange(wave_count, dtype=jnp.int32)
-    phase_turns = positions[:, None] * wavenumbers[None, :] % total_lon
-    phase_angle = phase_turns.astype(jnp.float32) * (2.0 * math.pi / total_lon)
-    valid_wave = (wavenumbers <= total_lon // 2)[None, :]
-    return (
-        jnp.where(valid_wave, jnp.cos(phase_angle), 0.0),
-        jnp.where(valid_wave, jnp.sin(phase_angle), 0.0),
-    )
-
-
-def wave_weights(cut_rows, total_lon, wave_count):
-    wavenumbers = jnp.arange(wave_count, dtype=jnp.int32)
-    double = jnp.where((wavenumbers == 0) | (2 * wavenumbers == total_lon), 1.0, 2.0)
-    kept_mask = (wavenumbers[None, :] <= cut_rows[:, None]) & (
-        wavenumbers[None, :] <= total_lon // 2
-    )
-    return jnp.where(kept_mask, double[None, :] / total_lon, 0.0)
+def split_table(table):
+    high = table.astype(jnp.bfloat16)
+    low = (table - high.astype(np.float64)).astype(jnp.bfloat16)
+    return high, low
+
+
+def filter_tables(blocks, width):
+    total = blocks * width
+    lanes = -(-width // 128) * 128
+    outer = np.arange(blocks)[:, None] * np.arange(blocks)[None, :] % blocks * (2 * np.pi / blocks)
+    forward = np.block([[np.cos(outer), np.sin(outer)], [-np.sin(outer), np.cos(outer)]])
+    middle = np.arange(blocks)[:, None] * np.arange(width)[None, :] * (2 * np.pi / total)
+    twiddle = np.zeros((2, blocks, lanes), np.float32)
+    twiddle[0, :, :width] = np.cos(middle)
+    twiddle[1, :, :width] = np.sin(middle)
+    inner = np.arange(width)[:, None] * np.arange(width)[None, :] % width * (2 * np.pi / width)
+    within = np.zeros((lanes, 2 * lanes))
+    within[:width, :width] = np.cos(inner)
+    within[:width, lanes : lanes + width] = np.sin(inner)
+    return (*split_table(forward), *split_table(forward.T), twiddle, *split_table(within))
+
+
+def split_value(value):
+    high = value.astype(jnp.bfloat16)
+    low = (value - high.astype(jnp.float32)).astype(jnp.bfloat16)
+    return high, low
+
+
+def mxu(left_side, right_side):
+    return jnp.dot(left_side, right_side, preferred_element_type=jnp.float32)
+
+
+def dot_left(table_high, table_low, value):
+    high, low = split_value(value)
+    return mxu(table_high, high) + (mxu(table_high, low) + mxu(table_low, high))
+
+
+def dot_right(value, table_high, table_low):
+    high, low = split_value(value)
+    return mxu(high, table_high) + (mxu(low, table_high) + mxu(high, table_low))
+
+
+def band_filter(values, cut, tables, blocks, width):
+    fwd_high, fwd_low, inv_high, inv_low, cos_mid, sin_mid, in_high, in_low = tables
+    lanes = values.shape[-1]
+    total = blocks * width
+    spread = dot_left(fwd_high, fwd_low, values)
+    real, imag = spread[:blocks], spread[blocks:]
+    turned = jnp.concatenate(
+        [real * cos_mid + imag * sin_mid, imag * cos_mid - real * sin_mid], axis=0
+    )
+    parts = dot_right(turned, in_high, in_low)
+    real = parts[:blocks, :lanes] + parts[blocks:, lanes:]
+    imag = parts[blocks:, :lanes] - parts[:blocks, lanes:]
+    wave = lax.broadcasted_iota(jnp.int32, (blocks, lanes), 0) + blocks * lax.broadcasted_iota(
+        jnp.int32, (blocks, lanes), 1
+    )
+    kept = jnp.minimum(wave, total - wave) <= cut
+    scale = jnp.where(kept, 1.0 / total, 0.0)
+    parts = dot_right(jnp.concatenate([real * scale, imag * scale], axis=0), in_high, in_low)
+    real = parts[:blocks, :lanes] - parts[blocks:, lanes:]
+    imag = parts[blocks:, :lanes] + parts[:blocks, lanes:]
+    turned = jnp.concatenate(
+        [real * cos_mid - imag * sin_mid, imag * cos_mid + real * sin_mid], axis=0
+    )
+    return dot_left(inv_high, inv_low, turned)
+
+
+def filter_kernel(cut_ref, values_ref, fh, fl, ih, il, tw, wh, wl, out_ref):
+    blocks = values_ref.shape[1]
+    lanes = tw.shape[2]
+    width = values_ref.shape[2]
+    pad = jnp.zeros((blocks, lanes - width), jnp.float32)
+    values = jnp.concatenate(
+        [
+            jnp.concatenate([values_ref[0], pad], axis=1),
+            jnp.concatenate([values_ref[1], pad], axis=1),
+        ],
+        axis=0,
+    )
+    tables = (fh[...], fl[...], ih[...], il[...], tw[0], tw[1], wh[...], wl[...])
+    out = band_filter(values, cut_ref[0], tables, blocks, width)
+    out_ref[0] = out[:blocks, :width]
+    out_ref[1] = out[blocks:, :width]
 
 
 def shards(tracer, zonal_wind, meridional_wind, polar_target, cutoff_wave):
@@ -144,22 +212,23 @@
     flat_count = slots_dev * levels
     flat_rows = slot_rows.reshape(flat_count, lon_dev)
     cut_rows = jnp.repeat(slot_cut, levels)
-    padded_waves = (total_lon // 2 + lon_count) // lon_count * lon_count
-    share_waves = padded_waves // lon_count
-    cosine_table, sine_table = spectral_tables(own_lon * lon_dev, lon_dev, total_lon, padded_waves)
-    part_cos = exact_dot(flat_rows, cosine_table)
-    part_sin = exact_dot(flat_rows, sine_table)
-    share_cos, share_sin = (
-        lax.psum_scatter(part_cos, "lon", scatter_dimension=1, tiled=True),
-        lax.psum_scatter(part_sin, "lon", scatter_dimension=1, tiled=True),
-    )
-    weights = wave_weights(cut_rows, total_lon, padded_waves)
-    share_weights = lax.dynamic_slice_in_dim(weights, own_lon * share_waves, share_waves, 1)
-    whole_cos, whole_sin = (
-        lax.all_gather(share_cos * share_weights, "lon", axis=1, tiled=True),
-        lax.all_gather(share_sin * share_weights, "lon", axis=1, tiled=True),
-    )
-    filtered_flat = dot_rows(whole_cos, cosine_table) + dot_rows(whole_sin, sine_table)
+    share = flat_count // lon_count
+    gathered = lax.all_to_all(
+        flat_rows.reshape(lon_count, share, lon_dev), "lon", split_axis=0, concat_axis=0, tiled=True
+    )
+    own_cut = lax.dynamic_slice_in_dim(cut_rows, own_lon * share, 1, 0)
+    tables = filter_tables(lon_count, lon_dev)
+    in_vmem = pl.BlockSpec(memory_space=pltpu.VMEM)
+    smoothed = pl.pallas_call(
+        filter_kernel,
+        out_shape=jax.ShapeDtypeStruct((share, lon_count, lon_dev), jnp.float32),
+        in_specs=[pl.BlockSpec(memory_space=pltpu.SMEM)] + [in_vmem] * 8,
+        out_specs=in_vmem,
+        name="band_filter",
+    )(own_cut, gathered.transpose(1, 0, 2), *[jnp.asarray(t) for t in tables])
+    filtered_flat = lax.all_to_all(
+        smoothed.transpose(1, 0, 2), "lon", split_axis=0, concat_axis=0, tiled=True
+    )
     filtered = filtered_flat.reshape(slots_dev, levels, lon_dev)
     back_send = jnp.einsum("sp,slx->plx", receive_select, filtered, precision=lax.Precision.HIGHEST)
     returned = lax.all_to_all(

time: 1110 us -> 239 us (0.22)
  the two profiles are of different devices: /device:TPU:1 before, /device:TPU:32 now
where the time goes in v1:
time: 239 us; the launch traced here: 238 us
  waiting for transfers between devices  112 us (47%)
  starting transfers between devices  82.9 us (35%)
  blocking collectives  26.7 us (11%)
  local copies, waits for them, and re-layouts  7.13 us (3%)
  Pallas kernels  3.33 us (1%)
  matrix products  2.6 us (1%)
  other arithmetic  2.44 us (1%)
    all_to_all x1, starting transfers between devices, shards(): lax.all_to_all(outgoing.reshape(lat_count, capacity, levels, lon_dev), 'l...  52.2 us
    all_to_all x1, waiting for transfers between devices, shards(): lax.all_to_all(outgoing.reshape(lat_count, capacity, levels, lon_dev), 'l...  46.3 us
    all_to_all x1, waiting for transfers between devices, shards(): lax.all_to_all(back_send.reshape(lat_count, capacity, levels, lon_dev), '...  46 us
    all_to_all x1, blocking collectives, shards(): lax.all_to_all(smoothed.transpose(1, 0, 2), 'lon', split_axis=0, concat_a...  26.7 us
    all_to_all x1, waiting for transfers between devices, shards(): lax.all_to_all(flat_rows.reshape(lon_count, share, lon_dev), 'lon', split...  18 us
    all_to_all x1, starting transfers between devices, shards(): lax.all_to_all(flat_rows.reshape(lon_count, share, lon_dev), 'lon', split...  16.1 us
    ppermute x2, starting transfers between devices, extended(): before = lax.ppermute(last, axis, up)  5.32 us
    ppermute x2, starting transfers between devices, extended(): after = lax.ppermute(initial, axis, down)  4.93 us
  transfers between devices with their start and end apart: 7, of which 5 were waited for; matrix products, arithmetic and copies ran while one was open for 1% of the time, Pallas kernels for 0%

profile of v1, /device:TPU:32, one launch (start us, length us, event | category | flops | bytes accessed | tf_op | source)
XLA Modules:
  0.0 238.1 jit_solution(17987708743242374865)
XLA Ops:
  0.6 1.0 fusion.22
  1.7 3.4 %collective-permute-start.2 = (f32[2,8,1,225]{3,2,1,0:T(1,128)S(1)}, f32[2,8,1,225]{3,2,1,0:T(1,128)S(1)}, u32[]{:S(2)}, u32[]{:S(2)}) collective-permute-start(f32[2,8,1,225]{3,2,1,0:T(1,128)S(1)} %get-tuple-element.12), channel_id=1, source_target_pairs={{0,1},{1,2},{2,3},{3,4},{4,5},{5,6},{6,7},{7,8},{8,9},{9,10},{10,1... | collective-permute-start | bytes 43208 | tf_op jit(solution)/shard_map/ppermute | solution.py:21
  5.1 1.3 collective-permute-start.3
  6.5 1.9 collective-permute-start
  8.4 3.6 %collective-permute-start.1 = (f32[2,8,24,1]{3,2,1,0:T(8,128)S(1)}, f32[2,8,24,1]{3,2,1,0:T(8,128)S(1)}, u32[]{:S(2)}, u32[]{:S(2)}) collective-permute-start(f32[2,8,24,1]{3,2,1,0:T(8,128)S(1)} %get-tuple-element.11), channel_id=1, source_target_pairs={{32,0},{64,32},{96,64},{128,96},{160,128},{192,160},{224,192},{256... | collective-permute-start | bytes 4616 | tf_op jit(solution)/shard_map/ppermute | solution.py:22
  12.2 0.7 copy-done.4
  13.5 1.8 collective-permute-done.1
  15.7 0.8 copy-done.2
  17.2 0.9 copy.27
  18.1 52.2 %all-to-all-start = ((f32[32,1,8,225]{3,2,1,0:T(8,128)}), f32[32,1,8,225]{3,2,1,0:T(8,128)S(1)}, u32[]{:S(2)}, u32[]{:S(2)}) async-start(f32[32,1,8,225]{3,2,1,0:T(8,128)} %copy.27), calls=%async_computation | async-start | bytes 524288 | tf_op jit(solution)/shard_map/all_to_all | solution.py:199
  70.6 46.3 %all-to-all-done = f32[32,1,8,225]{3,2,1,0:T(8,128)S(1)} async-done(((f32[32,1,8,225]{3,2,1,0:T(8,128)}), f32[32,1,8,225]{3,2,1,0:T(8,128)S(1)}, u32[]{:S(2)}, u32[]{:S(2)}) %all-to-all-start) | async-done | bytes 230432 | tf_op jit(solution)/shard_map/all_to_all | solution.py:199
  117.2 0.7 reshape_reshape.3
  117.9 16.1 %all-to-all-start.1 = ((f32[32,2,225]{2,1,0:T(2,128)}), f32[32,2,225]{2,1,0:T(2,128)S(1)}, u32[]{:S(2)}, u32[]{:S(2)}) async-start(f32[32,2,225]{2,1,0:T(2,128)} %reshape_reshape.3), calls=%async_computation.1 | async-start | bytes 131072 | tf_op jit(solution)/shard_map/all_to_all | solution.py:216
  134.0 0.7 copy-done.5
  135.0 0.6 dynamic_slice.3.cut_ref
  135.5 18.0 %all-to-all-done.1 = f32[32,2,225]{2,1,0:T(2,128)S(1)} async-done(((f32[32,2,225]{2,1,0:T(2,128)}), f32[32,2,225]{2,1,0:T(2,128)S(1)}, u32[]{:S(2)}, u32[]{:S(2)}) %all-to-all-start.1) | async-done | bytes 57632 | tf_op jit(solution)/shard_map/all_to_all | solution.py:216
  153.5 0.6 copy.46
  154.1 3.3 %band_filter.1 = f32[2,32,225]{2,1,0:T(8,128)} custom-call(s32[1]{0:T(128)} %dynamic_slice.3.cut_ref, f32[2,32,225]{2,1,0:T(8,128)} %bitcast.48, bf16[64,64]{1,0:T(8,128)(2,1)} %constant.87.clone.fh, bf16[64,64]{1,0:T(8,128)(2,1)} %constant.88.clone.fl, bf16[64,64]{1,0:T(8,128)(2,1)} %constant.89.clone.ih, bf16[64,64]{1,0:T(8,128)(2,1)} %constant.90.clone.il, ...), custom_call_target="tpu_custom_call" | custom-call | tf_op jit(solution)/shard_map/band_filter/pallas_call | solution.py:222
  157.5 0.9 copy.31
  158.4 26.7 %all_to_all.20 = f32[32,2,225]{2,1,0:T(2,128)S(1)} all-to-all(f32[32,2,225]{2,1,0:T(2,128)S(1)} %copy.31), channel_id=1, replica_groups=mesh['lon'=32,'lat'=32] {'lon'}, dimensions={0} | all-to-all | bytes 115200 | tf_op jit(solution)/shard_map/all_to_all | solution.py:229
  185.7 0.9 copy.33
  186.6 4.3 %all-to-all-start.3 = ((f32[32,1,8,225]{3,2,1,0:T(8,128)}), f32[32,1,8,225]{3,2,1,0:T(8,128)S(1)}, u32[]{:S(2)}, u32[]{:S(2)}) async-start(f32[32,1,8,225]{3,2,1,0:T(8,128)} %copy.33), calls=%async_computation.3 | async-start | bytes 524288 | tf_op jit(solution)/shard_map/all_to_all | solution.py:234
  191.1 46.0 %all-to-all-done.3 = f32[32,1,8,225]{3,2,1,0:T(8,128)S(1)} async-done(((f32[32,1,8,225]{3,2,1,0:T(8,128)}), f32[32,1,8,225]{3,2,1,0:T(8,128)S(1)}, u32[]{:S(2)}, u32[]{:S(2)}) %all-to-all-start.3) | async-done | bytes 230432 | tf_op jit(solution)/shard_map/all_to_all | solution.py:234
  237.1 1.1 fusion.1
  (41 shorter events, 3.6 us)
Async XLA Ops:
  0.6 5.7 %copy-start = (f32[8,24,225]{2,1,0:T(8,128)S(1)}, f32[8,24,225]{2,1,0:T(8,128)}, u32[]{:S(2)}) copy-start(f32[8,24,225]{2,1,0:T(8,128)} %param.12) | copy-start | bytes 518404
  0.6 5.7 %copy-start.1 = (f32[8,24,225]{2,1,0:T(8,128)S(1)}, f32[8,24,225]{2,1,0:T(8,128)}, u32[]{:S(2)}) copy-start(f32[8,24,225]{2,1,0:T(8,128)} %param.13) | copy-start | bytes 518404
  1.7 14.0 %collective-permute-start.2 = (f32[2,8,1,225]{3,2,1,0:T(1,128)S(1)}, f32[2,8,1,225]{3,2,1,0:T(1,128)S(1)}, u32[]{:S(2)}, u32[]{:S(2)}) collective-permute-start(f32[2,8,1,225]{3,2,1,0:T(1,128)S(1)} %get-tuple-element.12), channel_id=1, source_target_pairs={{0,1},{1,2},{2,3},{3,4},{4,5},{5,6},{6,7},{7,8},{8,9},{9,10},{10,1... | collective-permute-start | bytes 43208 | tf_op jit(solution)/shard_map/ppermute | solution.py:21
  5.1 10.6 %collective-permute-start.3 = (f32[2,8,1,225]{3,2,1,0:T(1,128)S(1)}, f32[2,8,1,225]{3,2,1,0:T(1,128)S(1)}, u32[]{:S(2)}, u32[]{:S(2)}) collective-permute-start(f32[2,8,1,225]{3,2,1,0:T(1,128)S(1)} %get-tuple-element.13), channel_id=1, source_target_pairs={{1,0},{2,1},{3,2},{4,3},{5,4},{6,5},{7,6},{8,7},{9,8},{10,9},{11,1... | collective-permute-start | bytes 43208 | tf_op jit(solution)/shard_map/ppermute | solution.py:22
  6.5 7.0 %collective-permute-start = (f32[2,8,24,1]{3,2,1,0:T(8,128)S(1)}, f32[2,8,24,1]{3,2,1,0:T(8,128)S(1)}, u32[]{:S(2)}, u32[]{:S(2)}) collective-permute-start(f32[2,8,24,1]{3,2,1,0:T(8,128)S(1)} %get-tuple-element.10), channel_id=1, source_target_pairs={{0,32},{32,64},{64,96},{96,128},{128,160},{160,192},{192,224},{224... | collective-permute-start | bytes 4616 | tf_op jit(solution)/shard_map/ppermute | solution.py:21
  8.4 6.8 %collective-permute-start.1 = (f32[2,8,24,1]{3,2,1,0:T(8,128)S(1)}, f32[2,8,24,1]{3,2,1,0:T(8,128)S(1)}, u32[]{:S(2)}, u32[]{:S(2)}) collective-permute-start(f32[2,8,24,1]{3,2,1,0:T(8,128)S(1)} %get-tuple-element.11), channel_id=1, source_target_pairs={{32,0},{64,32},{96,64},{128,96},{160,128},{192,160},{224,192},{256... | collective-permute-start | bytes 4616 | tf_op jit(solution)/shard_map/ppermute | solution.py:22
  12.2 0.7 copy-start.4
  15.5 0.9 copy-start.2
  18.1 98.8 %all-to-all-start = ((f32[32,1,8,225]{3,2,1,0:T(8,128)}), f32[32,1,8,225]{3,2,1,0:T(8,128)S(1)}, u32[]{:S(2)}, u32[]{:S(2)}) async-start(f32[32,1,8,225]{3,2,1,0:T(8,128)} %copy.27), calls=%async_computation | async-start | bytes 524288 | tf_op jit(solution)/shard_map/all_to_all | solution.py:199
  117.9 35.6 %all-to-all-start.1 = ((f32[32,2,225]{2,1,0:T(2,128)}), f32[32,2,225]{2,1,0:T(2,128)S(1)}, u32[]{:S(2)}, u32[]{:S(2)}) async-start(f32[32,2,225]{2,1,0:T(2,128)} %reshape_reshape.3), calls=%async_computation.1 | async-start | bytes 131072 | tf_op jit(solution)/shard_map/all_to_all | solution.py:216
  134.0 0.7 copy-start.5
  185.1 0.6 copy-start.3
  186.6 50.5 %all-to-all-start.3 = ((f32[32,1,8,225]{3,2,1,0:T(8,128)}), f32[32,1,8,225]{3,2,1,0:T(8,128)S(1)}, u32[]{:S(2)}, u32[]{:S(2)}) async-start(f32[32,1,8,225]{3,2,1,0:T(8,128)} %copy.33), calls=%async_computation.3 | async-start | bytes 524288 | tf_op jit(solution)/shard_map/all_to_all | solution.py:234

commit v2 on v0

v2 whole, which is shorter than its diff:
```python
import math

import jax
import jax.numpy as jnp
import numpy as np
from jax import lax
from jax.experimental import pallas as pl
from jax.experimental.pallas import tpu as pltpu
from jax.sharding import PartitionSpec as P

courant_number = 0.4
LEV, NLAT, NLON = 8, 768, 7200
NH, NPOLAR, SLOTS = 128, 256, 8
N_LAT, N_LON = 32, 32
ROWS, COLS, LANES = NLAT // N_LAT, NLON // N_LON, 256
FLAT = LEV * ROWS
SOURCES, PLACES = 6, 16
MESH = pl.DeviceIdType.MESH


def half_of(lat):
    return lax.rem(lax.div(lat, 4), 2)


def place_of(lat):
    return lax.div(lat, 8) * 4 + lax.rem(lat, 4)


def lat_of(place, half):
    return lax.div(place, 4) * 8 + half * 4 + lax.rem(place, 4)


def source_place(source, half):
    return jnp.where(source < 4 - 2 * half, source, source + 10)


def worker_lon(worker):
    return lax.div(8 * worker + 4, 3)


def worker_at(lon):
    worker = lax.div(3 * lon + 3, 8)
    return worker, 8 * worker + 4 <= 3 * lon + 2


def filter_tables():
    angle = np.arange(N_LON)[:, None] * np.arange(N_LON)[None, :] % N_LON * (2 * np.pi / N_LON)
    across = np.zeros((2, LEV // 2, N_LON, N_LON, LEV))
    for pair in range(LEV // 2):
        across[0, pair, :, :, 2 * pair] = np.cos(angle)
        across[0, pair, :, :, 2 * pair + 1] = np.sin(angle)
        across[1, pair, :, :, 2 * pair] = -np.sin(angle)
        across[1, pair, :, :, 2 * pair + 1] = np.cos(angle)
    across = across.reshape(LEV * N_LON, LEV * N_LON)
    middle = np.arange(N_LON)[:, None] * np.arange(COLS)[None, :] * (2 * np.pi / NLON)
    twiddle = np.zeros((2, N_LON, LANES), np.float32)
    twiddle[0, :, :COLS] = np.cos(middle)
    twiddle[1, :, :COLS] = np.sin(middle)
    inner = np.arange(COLS)[:, None] * np.arange(COLS)[None, :] % COLS * (2 * np.pi / COLS)
    within = np.zeros((LANES, 2 * LANES))
    within[:COLS, :COLS] = np.cos(inner)
    within[:COLS, LANES : LANES + COLS] = np.sin(inner)
    return [a.astype(np.float32) for a in (across, across.T, within, twiddle)]


def row_factors():
    row = np.arange(NLAT, dtype=np.float32)
    step = np.float32(math.pi / NLAT)
    face = np.sin(((row + np.float32(1.0)) * step).astype(np.float64)).astype(np.float32)
    face[-1] = 0.0
    centre = np.sin(((row + np.float32(0.5)) * step).astype(np.float64)).astype(np.float32)
    below = np.concatenate([np.zeros(1, np.float32), face[:-1]])
    table = np.stack([face, below, centre]).reshape(3, N_LAT, ROWS).transpose(1, 0, 2)
    return np.ascontiguousarray(np.broadcast_to(table[..., None], (N_LAT, 3, ROWS, 128)))


def routing_plan(polar_target, cutoff_wave):
    lat, lon = lax.axis_index("lat"), lax.axis_index("lon")
    half, place = half_of(lat), place_of(lat)
    index = np.arange(NPOLAR)
    glob = np.where(index < NH, index, index + NLAT - NPOLAR)
    home, own_row = glob // ROWS, glob % ROWS
    home_half, home_place = (home // 4) % 2, home // 8 * 4 + home % 4
    home_source = home_half * SOURCES + np.where(
        home_place < 4 - 2 * home_half, home_place, home_place - 10
    )
    home, own_row, home_source = (
        jnp.asarray(a, jnp.int32)[None, :] for a in (home, own_row, home_source)
    )
    target = polar_target[None, :]
    target_lat = target // SLOTS
    target_code = place_of(target_lat) * 2 + half_of(target_lat)
    worker, _ = worker_at(lon)
    worker_home = lat_of(source_place(lax.div(worker, 2), half), half)
    worker_target = place * 2 + lax.rem(worker, 2)
    entry = lax.broadcasted_iota(jnp.int32, (65, 1), 0)
    mine = home == lat
    value = jnp.where(
        entry < 32,
        jnp.where(mine & (target_code == entry), own_row, 0),
        jnp.where(
            entry < 56,
            jnp.where(mine & (own_row == entry - 32), target_code, 0),
            jnp.where(
                entry < 64,
                jnp.where(target == lat * SLOTS + entry - 56, home_source, 0),
                jnp.where(
                    (home == worker_home) & (target_code == worker_target), cutoff_wave[None, :], 0
                ),
            ),
        ),
    )
    return jnp.sum(value, axis=1)


def split_value(value):
    high = value.astype(jnp.bfloat16)
    low = (value - high.astype(jnp.float32)).astype(jnp.bfloat16)
    return high, low


def mxu(left_side, right_side):
    return jnp.dot(left_side, right_side, preferred_element_type=jnp.float32)


def dot_left(table_high, table_low, value):
    high, low = split_value(value)
    return mxu(table_high, high) + (mxu(table_high, low) + mxu(table_low, high))


def dot_right(value, table_high, table_low):
    high, low = split_value(value)
    return mxu(high, table_high) + (mxu(low, table_high) + mxu(high, table_low))


def band_filter(values, cut, tables):
    fwd_high, fwd_low, inv_high, inv_low, in_high, in_low, cos_mid, sin_mid = tables
    part = N_LON * LEV // 2
    spread = dot_left(fwd_high, fwd_low, values)
    real, imag = spread[:part], spread[part:]
    turned = jnp.concatenate(
        [real * cos_mid + imag * sin_mid, imag * cos_mid - real * sin_mid], axis=0
    )
    parts = dot_right(turned, in_high, in_low)
    real = parts[:part, :LANES] + parts[part:, LANES:]
    imag = parts[part:, :LANES] - parts[:part, LANES:]
    shape = (N_LON, LANES)
    wave = lax.broadcasted_iota(jnp.int32, shape, 0) + N_LON * lax.broadcasted_iota(
        jnp.int32, shape, 1
    )
    scale = jnp.where(jnp.minimum(wave, NLON - wave) <= cut, 1.0 / NLON, 0.0)
    scale = jnp.concatenate([scale] * (LEV // 2), axis=0)
    parts = dot_right(jnp.concatenate([real * scale, imag * scale], axis=0), in_high, in_low)
    real = parts[:part, :LANES] - parts[part:, LANES:]
    imag = parts[part:, :LANES] + parts[:part, LANES:]
    turned = jnp.concatenate(
        [real * cos_mid - imag * sin_mid, imag * cos_mid + real * sin_mid], axis=0
    )
    return dot_left(inv_high, inv_low, turned)


def each(count, step):
    lax.fori_loop(0, count, lambda k, carry: (step(k), carry)[1], 0)


def widened(block):
    pad = jnp.zeros((LEV, ROWS, LANES - COLS), jnp.float32)
    return jnp.concatenate([block, pad], axis=2).reshape(FLAT, LANES)


def spread_rows(edge):
    return jnp.broadcast_to(edge[:, None, :], (LEV, ROWS, LANES)).reshape(FLAT, LANES)


def substep_kernel(
    plan,
    tracer_hbm,
    zonal_hbm,
    merid_hbm,
    factor_hbm,
    forward_hbm,
    inverse_hbm,
    within_hbm,
    tw_hbm,
    next_out,
    slots_out,
    tracer,
    zonal,
    merid,
    factor,
    forward,
    inverse,
    within,
    fh,
    fl,
    ih,
    il,
    wh,
    wl,
    tw,
    lon_edge,
    east_in,
    west_in,
    south_edge,
    north_edge,
    south_in,
    north_in,
    increment,
    by_row,
    outbound,
    column,
    gathered,
    smoothed,
    returned,
    slot_in,
    homeward,
    load_sem,
    edge_send,
    edge_recv,
    out_send,
    out_recv,
    gather_send,
    gather_recv,
    back_send,
    back_recv,
    cross_send,
    cross_recv,
    home_send,
    home_recv,
):
    lon, lat = lax.axis_index("lon"), lax.axis_index("lat")
    half, place = half_of(lat), place_of(lat)
    first_places = 4 - 2 * half
    is_source = jnp.logical_or(place < first_places, place >= first_places + 10)
    source = jnp.where(place < first_places, place, place - 10)
    worker, is_worker = worker_at(lon)
    work_source, work_half = lax.div(worker, 2), lax.rem(worker, 2)
    across = jnp.logical_and(is_worker, work_half != half)
    east, west = lax.rem(lon + 1, N_LON), lax.rem(lon + N_LON - 1, N_LON)
    has_north, has_south = lat < N_LAT - 1, lat > 0

    loads = [
        pltpu.make_async_copy(a, b, load_sem.at[i])
        for i, (a, b) in enumerate(
            [
                (tracer_hbm, tracer),
                (zonal_hbm, zonal),
                (merid_hbm, merid),
                (factor_hbm.at[lat], factor),
                (forward_hbm, forward),
                (inverse_hbm, inverse),
                (within_hbm, within),
                (tw_hbm, tw),
            ]
        )
    ]
    for load in loads:
        load.start()

    barrier = pltpu.get_barrier_semaphore()

    def greet(to_lon, to_lat):
        pl.semaphore_signal(
            barrier, inc=1, device_id={"lon": to_lon, "lat": to_lat}, device_id_type=MESH
        )

    @pl.when(has_north)
    def _():
        greet(lon, lat + 1)

    @pl.when(has_south)
    def _():
        greet(lon, lat - 1)

    each(N_LON, lambda k: greet(k, lat_of(place, 1 - half)))
    each(N_LON - 1, lambda k: greet(lax.rem(lon + 1 + k, N_LON), lat))

    @pl.when(is_source)
    def _():
        each(PLACES - 1, lambda k: greet(lon, lat_of(lax.rem(place + 1 + k, PLACES), half)))

    @pl.when(jnp.logical_not(is_source))
    def _():
        each(SOURCES, lambda k: greet(lon, lat_of(source_place(k, half), half)))

    def send(what, where, send_sem, recv_sem, to_lon, to_lat):
        return pltpu.make_async_remote_copy(
            src_ref=what,
            dst_ref=where,
            send_sem=send_sem,
            recv_sem=recv_sem,
            device_id={"lon": to_lon, "lat": to_lat},
            device_id_type=MESH,
        )

    def take(where, recv_sem):
        send(where, where, recv_sem, recv_sem, lon, lat).wait_recv()

    def sent(what, send_sem):
        send(what, what, send_sem, send_sem, lon, lat).wait_send()

    for load in loads[:4]:
        load.wait()
    t = widened(tracer[...])
    u = widened(zonal[...])
    v = widened(merid[...])
    lane = lax.broadcasted_iota(jnp.int32, (FLAT, LANES), 1)
    row = lax.rem(lax.broadcasted_iota(jnp.int32, (FLAT, LANES), 0), ROWS)
    narrow = lane[:, :128]
    last = COLS - 1 - 128
    edge = jnp.where(
        narrow == 0,
        t[:, :128],
        jnp.where(
            narrow == 1,
            pltpu.roll(t[:, 128:], 128 + 1 - last, 1),
            pltpu.roll(u[:, 128:], 128 + 2 - last, 1),
        ),
    )
    edge = jnp.concatenate([edge, jnp.zeros((LANES - FLAT, 128), jnp.float32)], axis=0)
    lon_edge[...] = edge.T[:8]
    for level in range(LEV):
        top, bottom = level * ROWS + ROWS - 1, level * ROWS
        south_edge[0, level : level + 1, :] = t[top : top + 1]
        south_edge[1, level : level + 1, :] = v[top : top + 1]
        north_edge[level : level + 1, :] = t[bottom : bottom + 1]

    for load in loads[4:]:
        load.wait()

    @pl.when(is_worker)
    def _():
        fh[...], fl[...] = split_value(forward[...])
        ih[...], il[...] = split_value(inverse[...])
        wh[...], wl[...] = split_value(within[...])

    pl.semaphore_wait(
        barrier,
        2 * N_LON
        - 1
        + jnp.where(is_source, PLACES - 1, SOURCES)
        + jnp.where(has_north, 1, 0)
        + jnp.where(has_south, 1, 0),
    )

    @pl.when(has_north)
    def _():
        send(south_edge, south_in, edge_send.at[0], edge_recv.at[0], lon, lat + 1).start()

    @pl.when(has_south)
    def _():
        send(north_edge, north_in, edge_send.at[1], edge_recv.at[1], lon, lat - 1).start()

    send(lon_edge, west_in, edge_send.at[2], edge_recv.at[2], east, lat).start()
    send(lon_edge, east_in, edge_send.at[3], edge_recv.at[3], west, lat).start()

    @pl.when(jnp.logical_not(has_south))
    def _():
        south_in[...] = jnp.zeros(south_in.shape, jnp.float32)

    @pl.when(jnp.logical_not(has_north))
    def _():
        north_in[...] = jnp.zeros(north_in.shape, jnp.float32)

    take(west_in, edge_recv.at[2])
    take(east_in, edge_recv.at[3])
    columns = jnp.concatenate(
        [east_in[...], west_in[...], jnp.zeros((112, LANES), jnp.float32)], axis=0
    ).T[:FLAT]
    tracer_east, tracer_west, wind_west = columns[:, 0:1], columns[:, 9:10], columns[:, 10:11]
    shifted = jnp.where(lane == COLS - 1, tracer_east, pltpu.roll(t, LANES - 1, 1))
    east_flux = u * (t + shifted) * 0.5
    west_flux = jnp.where(lane == 0, wind_west * (tracer_west + t) * 0.5, pltpu.roll(east_flux, 1, 1))
    zonal_div = east_flux - west_flux

    @pl.when(has_south)
    def _():
        take(south_in, edge_recv.at[0])

    @pl.when(has_north)
    def _():
        take(north_in, edge_recv.at[1])

    def by_lane(i):
        rows = jnp.concatenate([factor[i], factor[i]], axis=1)
        return jnp.broadcast_to(rows[None], (LEV, ROWS, LANES)).reshape(FLAT, LANES)

    above = jnp.where(row == ROWS - 1, spread_rows(north_in[...]), pltpu.roll(t, FLAT - 1, 0))
    north_flux = v * by_lane(0) * (t + above) * 0.5
    below_flux = spread_rows(south_in[1]) * by_lane(1) * (spread_rows(south_in[0]) + t) * 0.5
    south_flux = jnp.where(row == 0, below_flux, pltpu.roll(north_flux, 1, 0))
    change = -courant_number * (zonal_div + (north_flux - south_flux) / by_lane(2))
    change = jnp.where(lane < COLS, change, 0.0)
    increment[...] = change

    @pl.when(is_source)
    def _():
        for level in range(LEV):
            by_row[:, level, :] = increment[level * ROWS : (level + 1) * ROWS, :]

        def leave(k):
            to = lax.rem(place + 1 + k, PLACES)
            outbound[2 * to] = by_row[plan[2 * to]]
            outbound[2 * to + 1] = by_row[plan[2 * to + 1]]
            send(
                outbound.at[pl.ds(2 * to, 2)],
                column.at[source],
                out_send,
                out_recv.at[source],
                lon,
                lat_of(to, half),
            ).start()

        each(PLACES - 1, leave)
        column[source, 0] = by_row[plan[2 * place]]
        column[source, 1] = by_row[plan[2 * place + 1]]

    def pass_on(s):
        @pl.when(jnp.logical_not(jnp.logical_and(is_source, source == s)))
        def _():
            take(column.at[s], out_recv.at[s])

        for t_half in range(2):
            to = worker_lon(2 * s + t_half)

            @pl.when(to != lon)
            def _():
                send(
                    column.at[s, t_half], gathered.at[lon], gather_send, gather_recv, to, lat
                ).start()

            @pl.when(to == lon)
            def _():
                gathered[lon] = column[s, t_half]

    each(SOURCES, pass_on)

    next_out[...] = tracer[...] + increment[...].reshape(LEV, ROWS, LANES)[:, :, :COLS]
    @pl.when(is_worker)
    def _():
        take(gathered.at[pl.ds(0, N_LON - 1)], gather_recv)
        cos_mid = jnp.concatenate([tw[0]] * (LEV // 2), axis=0)
        sin_mid = jnp.concatenate([tw[1]] * (LEV // 2), axis=0)
        tables = (fh[...], fl[...], ih[...], il[...], wh[...], wl[...], cos_mid, sin_mid)
        result = band_filter(gathered[...].reshape(N_LON * LEV, LANES), plan[64], tables)
        smoothed[...] = result.reshape(N_LON, LEV, LANES)

        @pl.when(across)
        def _():
            each(
                N_LON,
                lambda k: send(
                    smoothed.at[lax.rem(lon + k, N_LON)],
                    slot_in.at[half * SOURCES + work_source],
                    cross_send,
                    cross_recv,
                    lax.rem(lon + k, N_LON),
                    lat_of(place, 1 - half),
                ).start(),
            )

        each(
            N_LON - 1,
            lambda k: send(
                smoothed.at[lax.rem(lon + 1 + k, N_LON)],
                returned.at[work_source, work_half],
                back_send,
                back_recv.at[work_source],
                lax.rem(lon + 1 + k, N_LON),
                lat,
            ).start(),
        )
        returned[work_source, work_half] = smoothed[lon]

    def go_home(s):
        own = jnp.logical_and(is_worker, work_source == s)

        @pl.when(own)
        def _():
            take(returned.at[s, 0], back_recv.at[s])

        @pl.when(jnp.logical_not(own))
        def _():
            take(returned.at[s], back_recv.at[s])

        stays = jnp.logical_and(is_source, source == s)

        @pl.when(stays)
        def _():
            homeward[2 * place] = returned[s, 0]
            homeward[2 * place + 1] = returned[s, 1]

        @pl.when(jnp.logical_not(stays))
        def _():
            send(
                returned.at[s],
                homeward.at[pl.ds(2 * place, 2)],
                home_send,
                home_recv,
                lon,
                lat_of(source_place(s, half), half),
            ).start()

        slot_in[half * SOURCES + s] = returned[s, half]

    each(SOURCES, go_home)
    take(slot_in.at[pl.ds(0, SOURCES)], cross_recv)
    for slot in range(SLOTS):
        slots_out[slot] = slot_in[plan[56 + slot]][:, :COLS]

    @pl.when(is_source)
    def _():
        take(homeward.at[pl.ds(0, 2 * PLACES - 2)], home_recv)
        for j in range(ROWS):
            lat_row = lat * ROWS + j
            polar = jnp.logical_or(lat_row < NH, lat_row >= NLAT - NH)
            filtered = homeward[plan[32 + j]][:, :COLS]
            next_out[:, j, :] = jnp.where(polar, tracer[:, j, :] + filtered, next_out[:, j, :])

    @pl.when(has_north)
    def _():
        sent(south_edge, edge_send.at[0])

    @pl.when(has_south)
    def _():
        sent(north_edge, edge_send.at[1])

    sent(lon_edge, edge_send.at[2])
    sent(lon_edge, edge_send.at[3])

    @pl.when(is_source)
    def _():
        sent(outbound.at[pl.ds(0, 2 * PLACES - 2)], out_send)
        sent(homeward.at[pl.ds(0, 2 * SOURCES - 2)], home_send)

    @pl.when(jnp.logical_not(is_source))
    def _():
        sent(homeward.at[pl.ds(0, 2 * SOURCES)], home_send)

    @pl.when(is_worker)
    def _():
        sent(smoothed.at[pl.ds(0, 2 * SOURCES - 1)], gather_send)
        sent(smoothed.at[pl.ds(0, N_LON - 1)], back_send)

    @pl.when(jnp.logical_not(is_worker))
    def _():
        sent(smoothed.at[pl.ds(0, 2 * SOURCES)], gather_send)

    @pl.when(across)
    def _():
        sent(smoothed, cross_send)


def shards(tracer, zonal_wind, meridional_wind, polar_target, cutoff_wave):
    plan = routing_plan(polar_target, cutoff_wave)
    tables = [jnp.asarray(table) for table in filter_tables()]
    factors = jnp.asarray(row_factors())
    f32, bf16 = jnp.float32, jnp.bfloat16
    block = (LEV, ROWS, COLS)
    anywhere, in_vmem = pl.BlockSpec(memory_space=pltpu.HBM), pl.BlockSpec(memory_space=pltpu.VMEM)
    dma = pltpu.SemaphoreType.DMA
    square, wide = (LEV * N_LON, LEV * N_LON), (LANES, 2 * LANES)
    message = (LEV, LANES)
    return pl.pallas_call(
        substep_kernel,
        out_shape=(
            jax.ShapeDtypeStruct(block, f32),
            jax.ShapeDtypeStruct((SLOTS, LEV, COLS), f32),
        ),
        in_specs=[pl.BlockSpec(memory_space=pltpu.SMEM)] + [anywhere] * 8,
        out_specs=(in_vmem, in_vmem),
        scratch_shapes=[
            pltpu.VMEM(block, f32),
            pltpu.VMEM(block, f32),
            pltpu.VMEM(block, f32),
            pltpu.VMEM((3, ROWS, 128), f32),
            pltpu.VMEM(square, f32),
            pltpu.VMEM(square, f32),
            pltpu.VMEM(wide, f32),
            pltpu.VMEM(square, bf16),
            pltpu.VMEM(square, bf16),
            pltpu.VMEM(square, bf16),
            pltpu.VMEM(square, bf16),
            pltpu.VMEM(wide, bf16),
            pltpu.VMEM(wide, bf16),
            pltpu.VMEM((2, N_LON, LANES), f32),
            pltpu.VMEM(message, f32),
            pltpu.VMEM(message, f32),
            pltpu.VMEM(message, f32),
            pltpu.VMEM((2, *message), f32),
            pltpu.VMEM(message, f32),
            pltpu.VMEM((2, *message), f32),
            pltpu.VMEM(message, f32),
            pltpu.VMEM((FLAT, LANES), f32),
            pltpu.VMEM((ROWS, *message), f32),
            pltpu.VMEM((2 * PLACES, *message), f32),
            pltpu.VMEM((SOURCES, 2, *message), f32),
            pltpu.VMEM((N_LON, *message), f32),
            pltpu.VMEM((N_LON, *message), f32),
            pltpu.VMEM((SOURCES, 2, *message), f32),
            pltpu.VMEM((2 * SOURCES, *message), f32),
            pltpu.VMEM((2 * PLACES, *message), f32),
            dma((8,)),
            dma((4,)),
            dma((4,)),
            dma,
            dma((SOURCES,)),
            dma,
            dma,
            dma,
            dma((SOURCES,)),
            dma,
            dma,
            dma,
            dma,
        ],
        compiler_params=pltpu.CompilerParams(
            collective_id=0, has_side_effects=True, vmem_limit_bytes=60 * 2**20
        ),
        name="substep",
    )(plan, tracer, zonal_wind, meridional_wind, factors, *tables)


def solution(mesh):
    placed = (P(None, "lat", "lon"), P(None, "lat", "lon"), P(None, "lat", "lon"), P(), P())
    return jax.shard_map(
        shards,
        mesh=mesh,
        in_specs=placed,
        out_specs=(P(None, "lat", "lon"), P("lat", None, "lon")),
        check_vma=False,
    )
```

time: 1110 us -> 83.8 us (0.08)
  waiting for transfers between devices: 725 us -> 0 us
  blocking collectives: 194 us -> 0 us
  starting transfers between devices: 88.3 us -> 0 us
  Pallas kernels: 0 us -> 76.8 us
  matrix products: 68.5 us -> 0 us
  between operations: 15.4 us -> 0.69 us
    unnamed x2 -> x0, waiting for transfers between devices: 672 us -> none
    all_gather x2 -> x0, blocking collectives: 194 us -> none  [the longest x1 101 us: shards(): lax.all_gather(share_sin * share_weights, 'lon', axis=1, tiled=True)]
    pallas_call x0 -> x1, Pallas kernels: none -> 76.8 us  [shards(): pl.pallas_call(substep_kernel, out_shape=(jax.ShapeDtypeStruct(block, f32...]
    dot_general x10 -> x0, matrix products: 68.5 us -> none  [the longest x4 33.8 us: exact_dot(): jnp.dot(left_side, right_side, precision=lax.Precision.HIGHEST, preferred...]
    all_to_all x2 -> x0, starting transfers between devices: 67.6 us -> none  [the longest x1 46.8 us: shards(): lax.all_to_all(outgoing.reshape(lat_count, capacity, levels, lon_dev), 'l...]
    all_to_all x2 -> x0, waiting for transfers between devices: 53.1 us -> none  [the longest x1 27 us: shards(): lax.all_to_all(outgoing.reshape(lat_count, capacity, levels, lon_dev), 'l...]
    ppermute x4 -> x0, starting transfers between devices: 20.6 us -> none  [the longest x2 12.2 us: extended(): after = lax.ppermute(initial, axis, down)]
  transfers between devices with their start and end apart: 7 -> 0, of which waited for: 4 -> 0; matrix products, arithmetic and copies ran while one was open for 0% -> 0% of each run, Pallas kernels for 0% -> 0%
where the time goes in v2:
time: 83.8 us; the launch traced here: 83.5 us
  Pallas kernels  76.8 us (92%)
  local copies, waits for them, and re-layouts  3.09 us (4%)
  other arithmetic  2.89 us (3%)
    pallas_call x1, Pallas kernels, shards(): pl.pallas_call(substep_kernel, out_shape=(jax.ShapeDtypeStruct(block, f32...  76.8 us
    unnamed x2, local copies, waits for them, and re-layouts  3.09 us

profile of v2, /device:TPU:1, one launch (start us, length us, event | category | flops | bytes accessed | tf_op | source)
XLA Modules:
  0.0 83.5 jit_solution(4215609360494553979)
XLA Ops:
  0.7 0.7 broadcast_compare_fusion
  1.4 0.7 and_select_fusion
  2.1 1.5 %select_reduce_fusion.plan = s32[65]{0:T(128)} fusion(s32[256]{0:T(256)S(1)} %get-tuple-element.2, s32[256]{0:T(256)} %constant.89.clone, s32[256]{0:T(256)} %param.16, s32[256]{0:T(256)} %constant.88.clone, s32[256]{0:T(256)S(1)} %get-tuple-element.3, s32[65]{0:T(128)S(1)} %get-tuple-element.4, s32[65]{0:T(128)S(1)} %get-tuple-element.5, ...), kind=kLoop, calls=%fused_computation | loop fusion | flops 199615 | bytes 6351 | tf_op jit(solution)/shard_map/reduce_sum | solution.py:113
  3.6 76.8 %substep.1 = (f32[8,24,225]{2,1,0:T(8,128)}, f32[8,8,225]{2,1,0:T(8,128)}) custom-call(s32[65]{0:T(128)} %select_reduce_fusion.plan, f32[8,24,225]{2,1,0:T(8,128)} %tracer_hbm.1, f32[8,24,225]{2,1,0:T(8,128)} %zonal_hbm.1, f32[8,24,225]{2,1,0:T(8,128)} %merid_hbm.1, f32[32,3,24,128]{3,2,1,0:T(8,128)} %constant.94.clone.factor_hbm, ...), custom_call_target="tpu_custom_call" | custom-call | tf_op jit(solution)/shard_map/substep/pallas_call | solution.py:564
  80.4 1.6 %copy.17 = f32[8,24,225]{2,1,0:T(8,128)} copy(f32[8,24,225]{2,1,0:T(8,128)} %get-tuple-element.10) | data formatting | bytes 345600
  82.0 1.5 %copy.18 = f32[8,8,225]{2,1,0:T(8,128)} copy(f32[8,8,225]{2,1,0:T(8,128)} %get-tuple-element.11) | data formatting | bytes 115200
  (3 shorter events, 0.0 us)

commit v3 on v2

--- a/solution.py
+++ b/solution.py
@@ -15,6 +15,8 @@
 ROWS, COLS, LANES = NLAT // N_LAT, NLON // N_LON, 256
 FLAT = LEV * ROWS
 SOURCES, PLACES = 6, 16
+SEAM_LOW = (3, 27)
+SEAM_LON = 15
 MESH = pl.DeviceIdType.MESH
 
 
@@ -84,13 +86,19 @@
     home_source = home_half * SOURCES + np.where(
         home_place < 4 - 2 * home_half, home_place, home_place - 10
     )
-    home, own_row, home_source = (
-        jnp.asarray(a, jnp.int32)[None, :] for a in (home, own_row, home_source)
+    seam = np.zeros(NPOLAR, np.int32)
+    for pair, low in enumerate(SEAM_LOW):
+        for side in range(2):
+            row = (home == low + side) & (own_row == (0 if side else ROWS - 1))
+            home_source = np.where(row, 2 * SOURCES + 2 * pair + side, home_source)
+            seam[row] = 1
+    home, own_row, home_source, seam = (
+        jnp.asarray(a, jnp.int32)[None, :] for a in (home, own_row, home_source, seam)
     )
     target = polar_target[None, :]
     target_lat = target // SLOTS
     target_code = place_of(target_lat) * 2 + half_of(target_lat)
-    worker, _ = worker_at(lon)
+    worker, is_worker = worker_at(lon)
     worker_home = lat_of(source_place(lax.div(worker, 2), half), half)
     worker_target = place * 2 + lax.rem(worker, 2)
     entry = lax.broadcasted_iota(jnp.int32, (65, 1), 0)
@@ -100,17 +108,30 @@
         jnp.where(mine & (target_code == entry), own_row, 0),
         jnp.where(
             entry < 56,
-            jnp.where(mine & (own_row == entry - 32), target_code, 0),
+            jnp.where(mine & (own_row == entry - 32), jnp.where(seam == 1, 2 * PLACES, target_code), 0),
             jnp.where(
                 entry < 64,
                 jnp.where(target == lat * SLOTS + entry - 56, home_source, 0),
                 jnp.where(
-                    (home == worker_home) & (target_code == worker_target), cutoff_wave[None, :], 0
+                    jnp.where(
+                        is_worker,
+                        (home == worker_home) & (target_code == worker_target),
+                        mine & (seam == 1),
+                    ),
+                    cutoff_wave[None, :],
+                    0,
                 ),
             ),
         ),
     )
     return jnp.sum(value, axis=1)
+
+
+def is_any(value, choices):
+    found = value == choices[0]
+    for choice in choices[1:]:
+        found = jnp.logical_or(found, value == choice)
+    return found
 
 
 def split_value(value):
@@ -157,6 +178,19 @@
         [real * cos_mid - imag * sin_mid, imag * cos_mid + real * sin_mid], axis=0
     )
     return dot_left(inv_high, inv_low, turned)
+
+
+def with_edge_terms(values):
+    low, high = values[:, :128], values[:, 128:]
+    lane = lax.broadcasted_iota(jnp.int32, low.shape, 1)
+    last = COLS - 1 - 128
+    count = values.shape[0]
+    next_first = pltpu.roll(pltpu.roll(high, 1, 1), count - LEV, 0)
+    product = high * next_first
+    flux = pltpu.roll(pltpu.roll(high, 127, 1) + product, 128 - (last + 2), 1)
+    low = jnp.where(lane == 0, low + pltpu.roll(flux, LEV, 0), low)
+    high = jnp.where(lane == last, high - pltpu.roll(product, 126, 1), high)
+    return jnp.concatenate([low, jnp.where(lane <= last, high, 0.0)], axis=1)
 
 
 def each(count, step):
@@ -214,6 +248,9 @@
     returned,
     slot_in,
     homeward,
+    seam_own,
+    seam_other,
+    seam_result,
     load_sem,
     edge_send,
     edge_recv,
@@ -227,6 +264,12 @@
     cross_recv,
     home_send,
     home_recv,
+    seam_send,
+    seam_recv,
+    seam_back_send,
+    seam_back_recv,
+    seam_out_send,
+    seam_out_recv,
 ):
     lon, lat = lax.axis_index("lon"), lax.axis_index("lat")
     half, place = half_of(lat), place_of(lat)
@@ -237,7 +280,15 @@
     work_source, work_half = lax.div(worker, 2), lax.rem(worker, 2)
     across = jnp.logical_and(is_worker, work_half != half)
     east, west = lax.rem(lon + 1, N_LON), lax.rem(lon + N_LON - 1, N_LON)
-    has_north, has_south = lat < N_LAT - 1, lat > 0
+    low_seam = is_any(lat, SEAM_LOW)
+    high_seam = is_any(lat, [low + 1 for low in SEAM_LOW])
+    at_seam = jnp.logical_or(low_seam, high_seam)
+    seam_side = jnp.where(high_seam, 1, 0)
+    other_lat = jnp.where(high_seam, lat - 1, lat + 1)
+    seam_worker = jnp.logical_and(at_seam, lon == SEAM_LON)
+    has_north = jnp.logical_and(lat < N_LAT - 1, jnp.logical_not(low_seam))
+    has_south = jnp.logical_and(lat > 0, jnp.logical_not(high_seam))
+    all_polar = jnp.logical_or(lat * ROWS + ROWS <= NH, lat * ROWS >= NLAT - NH)
 
     loads = [
         pltpu.make_async_copy(a, b, load_sem.at[i])
@@ -283,6 +334,14 @@
     def _():
         each(SOURCES, lambda k: greet(lon, lat_of(source_place(k, half), half)))
 
+    @pl.when(at_seam)
+    def _():
+        greet(SEAM_LON, other_lat)
+
+        @pl.when(seam_worker)
+        def _():
+            each(N_LON, lambda k: greet(lax.rem(lon + k, N_LON), other_lat))
+
     def send(what, where, send_sem, recv_sem, to_lon, to_lat):
         return pltpu.make_async_remote_copy(
             src_ref=what,
@@ -305,7 +364,6 @@
     u = widened(zonal[...])
     v = widened(merid[...])
     lane = lax.broadcasted_iota(jnp.int32, (FLAT, LANES), 1)
-    row = lax.rem(lax.broadcasted_iota(jnp.int32, (FLAT, LANES), 0), ROWS)
     narrow = lane[:, :128]
     last = COLS - 1 - 128
     edge = jnp.where(
@@ -328,7 +386,7 @@
     for load in loads[4:]:
         load.wait()
 
-    @pl.when(is_worker)
+    @pl.when(jnp.logical_or(is_worker, seam_worker))
     def _():
         fh[...], fl[...] = split_value(forward[...])
         ih[...], il[...] = split_value(inverse[...])
@@ -340,7 +398,9 @@
         - 1
         + jnp.where(is_source, PLACES - 1, SOURCES)
         + jnp.where(has_north, 1, 0)
-        + jnp.where(has_south, 1, 0),
+        + jnp.where(has_south, 1, 0)
+        + jnp.where(at_seam, 1, 0)
+        + jnp.where(seam_worker, N_LON, 0),
     )
 
     @pl.when(has_north)
@@ -351,8 +411,22 @@
     def _():
         send(north_edge, north_in, edge_send.at[1], edge_recv.at[1], lon, lat - 1).start()
 
-    send(lon_edge, west_in, edge_send.at[2], edge_recv.at[2], east, lat).start()
-    send(lon_edge, east_in, edge_send.at[3], edge_recv.at[3], west, lat).start()
+    @pl.when(jnp.logical_not(all_polar))
+    def _():
+        send(lon_edge, west_in, edge_send.at[2], edge_recv.at[2], east, lat).start()
+        send(lon_edge, east_in, edge_send.at[3], edge_recv.at[3], west, lat).start()
+
+    @pl.when(low_seam)
+    def _():
+        send(
+            south_edge, seam_other.at[lon], seam_send.at[0], seam_recv.at[0], SEAM_LON, other_lat
+        ).start()
+
+    @pl.when(high_seam)
+    def _():
+        send(
+            north_edge, seam_other.at[lon, 0], seam_send.at[0], seam_recv.at[0], SEAM_LON, other_lat
+        ).start()
 
     @pl.when(jnp.logical_not(has_south))
     def _():
@@ -361,42 +435,63 @@
     @pl.when(jnp.logical_not(has_north))
     def _():
         north_in[...] = jnp.zeros(north_in.shape, jnp.float32)
-
-    take(west_in, edge_recv.at[2])
-    take(east_in, edge_recv.at[3])
-    columns = jnp.concatenate(
-        [east_in[...], west_in[...], jnp.zeros((112, LANES), jnp.float32)], axis=0
-    ).T[:FLAT]
-    tracer_east, tracer_west, wind_west = columns[:, 0:1], columns[:, 9:10], columns[:, 10:11]
-    shifted = jnp.where(lane == COLS - 1, tracer_east, pltpu.roll(t, LANES - 1, 1))
-    east_flux = u * (t + shifted) * 0.5
-    west_flux = jnp.where(lane == 0, wind_west * (tracer_west + t) * 0.5, pltpu.roll(east_flux, 1, 1))
-    zonal_div = east_flux - west_flux
-
-    @pl.when(has_south)
-    def _():
-        take(south_in, edge_recv.at[0])
-
-    @pl.when(has_north)
-    def _():
-        take(north_in, edge_recv.at[1])
 
     def by_lane(i):
         rows = jnp.concatenate([factor[i], factor[i]], axis=1)
         return jnp.broadcast_to(rows[None], (LEV, ROWS, LANES)).reshape(FLAT, LANES)
 
-    above = jnp.where(row == ROWS - 1, spread_rows(north_in[...]), pltpu.roll(t, FLAT - 1, 0))
-    north_flux = v * by_lane(0) * (t + above) * 0.5
-    below_flux = spread_rows(south_in[1]) * by_lane(1) * (spread_rows(south_in[0]) + t) * 0.5
-    south_flux = jnp.where(row == 0, below_flux, pltpu.roll(north_flux, 1, 0))
-    change = -courant_number * (zonal_div + (north_flux - south_flux) / by_lane(2))
-    change = jnp.where(lane < COLS, change, 0.0)
-    increment[...] = change
+    def change_within():
+        @pl.when(has_south)
+        def _():
+            take(south_in, edge_recv.at[0])
+
+        @pl.when(has_north)
+        def _():
+            take(north_in, edge_recv.at[1])
+
+        t, u, v = widened(tracer[...]), widened(zonal[...]), widened(merid[...])
+        row = lax.rem(lax.broadcasted_iota(jnp.int32, (FLAT, LANES), 0), ROWS)
+        lane = lax.broadcasted_iota(jnp.int32, (FLAT, LANES), 1)
+        east_flux = u * (t + pltpu.roll(t, LANES - 1, 1)) * 0.5
+        zonal_div = east_flux - pltpu.roll(east_flux, 1, 1)
+        above = jnp.where(row == ROWS - 1, spread_rows(north_in[...]), pltpu.roll(t, FLAT - 1, 0))
+        north_flux = v * by_lane(0) * (t + above) * 0.5
+        below_flux = spread_rows(south_in[1]) * by_lane(1) * (spread_rows(south_in[0]) + t) * 0.5
+        south_flux = jnp.where(row == 0, below_flux, pltpu.roll(north_flux, 1, 0))
+        change = -courant_number * (zonal_div + (north_flux - south_flux) / by_lane(2))
+        return t, u, jnp.where(lane < COLS, change, 0.0), lane
 
     @pl.when(is_source)
     def _():
+        t, u, change, lane = change_within()
+        increment[...] = change
+        last_wind = 0.5 * courant_number * u[:, COLS - 1 : COLS]
+        marked = jnp.where(lane == COLS, t[:, 0:1], change)
+        marked = jnp.where(lane == COLS + 1, last_wind, marked)
+        marked = jnp.where(lane == COLS + 2, last_wind * t[:, COLS - 1 : COLS], marked)
         for level in range(LEV):
-            by_row[:, level, :] = increment[level * ROWS : (level + 1) * ROWS, :]
+            by_row[:, level, :] = marked[level * ROWS : (level + 1) * ROWS, :]
+
+        @pl.when(low_seam)
+        def _():
+            seam_own[lon, 0] = by_row[ROWS - 1]
+            seam_own[lon, 1] = south_edge[1]
+
+        @pl.when(high_seam)
+        def _():
+            seam_own[lon, 0] = by_row[0]
+            seam_own[lon, 1] = north_edge[...]
+
+        @pl.when(jnp.logical_and(at_seam, lon != SEAM_LON))
+        def _():
+            send(
+                seam_own.at[lon],
+                seam_own.at[lon],
+                seam_send.at[1],
+                seam_recv.at[1],
+                SEAM_LON,
+                lat,
+            ).start()
 
         def leave(k):
             to = lax.rem(place + 1 + k, PLACES)
@@ -435,16 +530,60 @@
 
     each(SOURCES, pass_on)
 
-    next_out[...] = tracer[...] + increment[...].reshape(LEV, ROWS, LANES)[:, :, :COLS]
+    @pl.when(jnp.logical_not(is_source))
+    def _():
+        increment[...] = change_within()[2]
+
+    @pl.when(jnp.logical_not(all_polar))
+    def _():
+        take(west_in, edge_recv.at[2])
+        take(east_in, edge_recv.at[3])
+        columns = jnp.concatenate(
+            [east_in[...], west_in[...], jnp.zeros((112, LANES), jnp.float32)], axis=0
+        ).T[:FLAT]
+        tracer_east, tracer_west, wind_west = columns[:, 0:1], columns[:, 9:10], columns[:, 10:11]
+        t, u = widened(tracer[...]), widened(zonal[...])
+        lane = lax.broadcasted_iota(jnp.int32, (FLAT, LANES), 1)
+        half_courant = 0.5 * courant_number
+        change = increment[...]
+        change = jnp.where(lane == COLS - 1, change - half_courant * (u * tracer_east), change)
+        change = jnp.where(lane == 0, change + half_courant * (wind_west * (tracer_west + t)), change)
+        next_out[...] = (t + change).reshape(LEV, ROWS, LANES)[:, :, :COLS]
+
+    @pl.when(seam_worker)
+    def _():
+        take(seam_own.at[pl.ds(0, N_LON - 1)], seam_recv.at[1])
+
+        @pl.when(low_seam)
+        def _():
+            take(seam_other.at[pl.ds(0, N_LON // 2)], seam_recv.at[0])
+            scale = -0.5 * courant_number * factor[0, ROWS - 1 :, :] / factor[2, ROWS - 1 :, :]
+            scale = jnp.concatenate([scale, scale], axis=1)[None]
+            gathered[...] = seam_own[:, 0] + scale * seam_own[:, 1] * seam_other[:, 0]
+
+        @pl.when(high_seam)
+        def _():
+            take(seam_other, seam_recv.at[0])
+            scale = 0.5 * courant_number * factor[1, :1, :] / factor[2, :1, :]
+            scale = jnp.concatenate([scale, scale], axis=1)[None]
+            gathered[...] = seam_own[:, 0] + scale * seam_other[:, 1] * (
+                seam_other[:, 0] + seam_own[:, 1]
+            )
+
     @pl.when(is_worker)
     def _():
         take(gathered.at[pl.ds(0, N_LON - 1)], gather_recv)
+
+    @pl.when(jnp.logical_or(is_worker, seam_worker))
+    def _():
         cos_mid = jnp.concatenate([tw[0]] * (LEV // 2), axis=0)
         sin_mid = jnp.concatenate([tw[1]] * (LEV // 2), axis=0)
         tables = (fh[...], fl[...], ih[...], il[...], wh[...], wl[...], cos_mid, sin_mid)
-        result = band_filter(gathered[...].reshape(N_LON * LEV, LANES), plan[64], tables)
-        smoothed[...] = result.reshape(N_LON, LEV, LANES)
-
+        values = with_edge_terms(gathered[...].reshape(N_LON * LEV, LANES))
+        smoothed[...] = band_filter(values, plan[64], tables).reshape(N_LON, LEV, LANES)
+
+    @pl.when(is_worker)
+    def _():
         @pl.when(across)
         def _():
             each(
@@ -472,6 +611,56 @@
         )
         returned[work_source, work_half] = smoothed[lon]
 
+    @pl.when(seam_worker)
+    def _():
+        each(
+            N_LON,
+            lambda k: send(
+                smoothed.at[lax.rem(lon + k, N_LON)],
+                seam_result.at[seam_side],
+                seam_back_send.at[0],
+                seam_back_recv,
+                lax.rem(lon + k, N_LON),
+                other_lat,
+            ).start(),
+        )
+        each(
+            N_LON - 1,
+            lambda k: send(
+                smoothed.at[lax.rem(lon + 1 + k, N_LON)],
+                seam_result.at[seam_side],
+                seam_back_send.at[1],
+                seam_back_recv,
+                lax.rem(lon + 1 + k, N_LON),
+                lat,
+            ).start(),
+        )
+        seam_result[seam_side] = smoothed[lon]
+
+    seam_pair = jnp.where(lat < NLAT // ROWS // 2, 0, 1)
+    seam_slots = [slot_in.at[pl.ds(2 * SOURCES + 2 * pair, 2)] for pair in range(2)]
+
+    @pl.when(at_seam)
+    def _():
+        @pl.when(seam_worker)
+        def _():
+            take(seam_result.at[0], seam_back_recv)
+
+        @pl.when(jnp.logical_not(seam_worker))
+        def _():
+            take(seam_result, seam_back_recv)
+
+        own_slots = slot_in.at[pl.ds(2 * SOURCES + 2 * seam_pair, 2)]
+
+        def spread(k):
+            to = lat_of(lax.rem(place + 1 + k, PLACES), half)
+            send(seam_result, own_slots, seam_out_send, seam_out_recv.at[seam_pair], lon, to).start()
+
+        each(PLACES - 1, spread)
+        slot_in[2 * SOURCES + 2 * seam_pair] = seam_result[0]
+        slot_in[2 * SOURCES + 2 * seam_pair + 1] = seam_result[1]
+        homeward[2 * PLACES] = seam_result[seam_side]
+
     def go_home(s):
         own = jnp.logical_and(is_worker, work_source == s)
 
@@ -505,6 +694,12 @@
 
     each(SOURCES, go_home)
     take(slot_in.at[pl.ds(0, SOURCES)], cross_recv)
+    for pair in range(2):
+
+        @pl.when(jnp.logical_not(jnp.logical_and(at_seam, seam_pair == pair)))
+        def _(pair=pair):
+            take(seam_slots[pair], seam_out_recv.at[pair])
+
     for slot in range(SLOTS):
         slots_out[slot] = slot_in[plan[56 + slot]][:, :COLS]
 
@@ -525,8 +720,31 @@
     def _():
         sent(north_edge, edge_send.at[1])
 
-    sent(lon_edge, edge_send.at[2])
-    sent(lon_edge, edge_send.at[3])
+    @pl.when(jnp.logical_not(all_polar))
+    def _():
+        sent(lon_edge, edge_send.at[2])
+        sent(lon_edge, edge_send.at[3])
+
+    @pl.when(low_seam)
+    def _():
+        sent(south_edge, seam_send.at[0])
+
+    @pl.when(high_seam)
+    def _():
+        sent(north_edge, seam_send.at[0])
+
+    @pl.when(at_seam)
+    def _():
+        sent(homeward.at[pl.ds(0, 2 * PLACES - 2)], seam_out_send)
+
+        @pl.when(jnp.logical_not(seam_worker))
+        def _():
+            sent(seam_own.at[lon], seam_send.at[1])
+
+        @pl.when(seam_worker)
+        def _():
+            sent(smoothed, seam_back_send.at[0])
+            sent(smoothed.at[pl.ds(0, N_LON - 1)], seam_back_send.at[1])
 
     @pl.when(is_source)
     def _():
@@ -598,8 +816,11 @@
             pltpu.VMEM((N_LON, *message), f32),
             pltpu.VMEM((N_LON, *message), f32),
             pltpu.VMEM((SOURCES, 2, *message), f32),
-            pltpu.VMEM((2 * SOURCES, *message), f32),
-            pltpu.VMEM((2 * PLACES, *message), f32),
+            pltpu.VMEM((2 * SOURCES + 4, *message), f32),
+            pltpu.VMEM((2 * PLACES + 1, *message), f32),
+            pltpu.VMEM((N_LON, 2, *message), f32),
+            pltpu.VMEM((N_LON, 2, *message), f32),
+            pltpu.VMEM((2, *message), f32),
             dma((8,)),
             dma((4,)),
             dma((4,)),
@@ -613,6 +834,12 @@
             dma,
             dma,
             dma,
+            dma((2,)),
+            dma((2,)),
+            dma((2,)),
+            dma,
+            dma,
+            dma((2,)),
         ],
         compiler_params=pltpu.CompilerParams(
             collective_id=0, has_side_effects=True, vmem_limit_bytes=60 * 2**20

time: 83.8 us -> 83.1 us (level)
  the two profiles are of different devices: /device:TPU:1 before, /device:TPU:6 now
where the time goes in v3:
time: 83.1 us; the launch traced here: 82.8 us
  Pallas kernels  75.4 us (91%)
  other arithmetic  3.59 us (4%)
  local copies, waits for them, and re-layouts  3.09 us (4%)
    pallas_call x1, Pallas kernels, shards(): pl.pallas_call(substep_kernel, out_shape=(jax.ShapeDtypeStruct(block, f32...  75.4 us
    unnamed x2, local copies, waits for them, and re-layouts  3.09 us

profile of v3, /device:TPU:6, one launch (start us, length us, event | category | flops | bytes accessed | tf_op | source)
XLA Modules:
  0.0 82.8 jit_solution(2728961297123050605)
XLA Ops:
  0.7 0.7 broadcast_compare_fusion
  1.4 0.7 broadcast_select_fusion
  2.1 0.7 select_select_fusion
  2.8 1.4 %select_reduce_fusion.plan = s32[65]{0:T(128)} fusion(s32[256]{0:T(256)S(1)} %select_select_fusion, s32[256]{0:T(256)} %constant.93.clone, s32[256]{0:T(256)} %param.17, s32[256]{0:T(256)S(1)} %get-tuple-element.2, s32[256]{0:T(256)} %constant.92.clone, s32[256]{0:T(256)S(1)} %get-tuple-element.3, s32[65]{0:T(128)S(1)} %get-tuple-element.4, ...), kind=kLoop, calls=%fused_computation | loop fusion | flops 199615 | bytes 7375 | tf_op jit(solution)/shard_map/reduce_sum | solution.py:127
  4.3 75.4 %substep.1 = (f32[8,24,225]{2,1,0:T(8,128)}, f32[8,8,225]{2,1,0:T(8,128)}) custom-call(s32[65]{0:T(128)} %select_reduce_fusion.plan, f32[8,24,225]{2,1,0:T(8,128)} %tracer_hbm.1, f32[8,24,225]{2,1,0:T(8,128)} %zonal_hbm.1, f32[8,24,225]{2,1,0:T(8,128)} %merid_hbm.1, f32[32,3,24,128]{3,2,1,0:T(8,128)} %constant.99.clone.factor_hbm, ...), custom_call_target="tpu_custom_call" | custom-call | tf_op jit(solution)/shard_map/substep/pallas_call | solution.py:782
  79.7 1.6 %copy.18 = f32[8,24,225]{2,1,0:T(8,128)} copy(f32[8,24,225]{2,1,0:T(8,128)} %get-tuple-element.10) | data formatting | bytes 345600
  81.3 1.5 %copy.19 = f32[8,8,225]{2,1,0:T(8,128)} copy(f32[8,8,225]{2,1,0:T(8,128)} %get-tuple-element.11) | data formatting | bytes 115200
  (3 shorter events, 0.0 us)

commit v4 on v3

--- a/solution.py
+++ b/solution.py
@@ -17,6 +17,8 @@
 SOURCES, PLACES = 6, 16
 SEAM_LOW = (3, 27)
 SEAM_LON = 15
+WORKERS_FROM = 4
+ENTRIES = 72
 MESH = pl.DeviceIdType.MESH
 
 
@@ -37,12 +39,23 @@
 
 
 def worker_lon(worker):
-    return lax.div(8 * worker + 4, 3)
+    return 2 * worker + WORKERS_FROM
 
 
 def worker_at(lon):
-    worker = lax.div(3 * lon + 3, 8)
-    return worker, 8 * worker + 4 <= 3 * lon + 2
+    worker = lax.div(lon + 32 - WORKERS_FROM, 2) - 16
+    found = jnp.logical_and(lon >= WORKERS_FROM, lon < WORKERS_FROM + 4 * SOURCES)
+    return worker, jnp.logical_and(found, lax.rem(lon - WORKERS_FROM + 32, 2) == 0)
+
+
+def alternate(lon, k):
+    step = lax.div(k + 1, 2)
+    return lax.rem(lon + N_LON + jnp.where(lax.rem(k, 2) == 1, step, -step), N_LON)
+
+
+def inward(k):
+    step = lax.div(k, 2)
+    return jnp.where(lax.rem(k, 2) == 1, N_LON - 1 - step, step)
 
 
 def filter_tables():
@@ -76,9 +89,7 @@
     return np.ascontiguousarray(np.broadcast_to(table[..., None], (N_LAT, 3, ROWS, 128)))
 
 
-def routing_plan(polar_target, cutoff_wave):
-    lat, lon = lax.axis_index("lat"), lax.axis_index("lon")
-    half, place = half_of(lat), place_of(lat)
+def polar_row_table():
     index = np.arange(NPOLAR)
     glob = np.where(index < NH, index, index + NLAT - NPOLAR)
     home, own_row = glob // ROWS, glob % ROWS
@@ -92,39 +103,31 @@
             row = (home == low + side) & (own_row == (0 if side else ROWS - 1))
             home_source = np.where(row, 2 * SOURCES + 2 * pair + side, home_source)
             seam[row] = 1
-    home, own_row, home_source, seam = (
-        jnp.asarray(a, jnp.int32)[None, :] for a in (home, own_row, home_source, seam)
-    )
-    target = polar_target[None, :]
-    target_lat = target // SLOTS
-    target_code = place_of(target_lat) * 2 + half_of(target_lat)
+    return np.stack([home, own_row, home_source, seam] * 2).astype(np.int32)
+
+
+def routing_plan(target, cutoff, rows, lon, lat):
+    half, place = half_of(lat), place_of(lat)
+    home, own_row, home_source, seam = (rows[i : i + 1] for i in range(4))
+    target = jnp.concatenate([target[0:1], target[1:2]], axis=1)
+    cutoff = jnp.concatenate([cutoff[0:1], cutoff[1:2]], axis=1)
+    target_lat = target >> 3
+    target_code = ((target_lat >> 3) * 4 + (target_lat & 3)) * 2 + ((target_lat >> 2) & 1)
     worker, is_worker = worker_at(lon)
-    worker_home = lat_of(source_place(lax.div(worker, 2), half), half)
-    worker_target = place * 2 + lax.rem(worker, 2)
-    entry = lax.broadcasted_iota(jnp.int32, (65, 1), 0)
+    worker_home = jnp.where(is_worker, lat_of(source_place(lax.div(worker, 2), half), half), lat)
+    worker_target = jnp.where(is_worker, place * 2 + lax.rem(worker, 2), -1)
+    entry = lax.broadcasted_iota(jnp.int32, (ENTRIES, NPOLAR), 0)
+    none = jnp.zeros((ENTRIES, NPOLAR), jnp.int32)
+    row_target = jnp.where(seam == 1, 2 * PLACES, target_code)
+    filtered_code = jnp.where(is_worker, target_code, jnp.where(seam == 1, -1, 0))
     mine = home == lat
-    value = jnp.where(
-        entry < 32,
-        jnp.where(mine & (target_code == entry), own_row, 0),
-        jnp.where(
-            entry < 56,
-            jnp.where(mine & (own_row == entry - 32), jnp.where(seam == 1, 2 * PLACES, target_code), 0),
-            jnp.where(
-                entry < 64,
-                jnp.where(target == lat * SLOTS + entry - 56, home_source, 0),
-                jnp.where(
-                    jnp.where(
-                        is_worker,
-                        (home == worker_home) & (target_code == worker_target),
-                        mine & (seam == 1),
-                    ),
-                    cutoff_wave[None, :],
-                    0,
-                ),
-            ),
-        ),
-    )
-    return jnp.sum(value, axis=1)
+    filtered_here = jnp.where((home == worker_home) & (filtered_code == worker_target), cutoff, 0)
+    leaving = jnp.where(mine & (target_code == entry), own_row, none)
+    landing = jnp.where(mine & (own_row == entry - 32), row_target, none)
+    slot = jnp.where(target == lat * SLOTS + entry - 56, home_source, none)
+    value = jnp.where(entry < 32, leaving, jnp.where(entry < 56, landing, slot))
+    value = jnp.where(entry < 64, value, jnp.where(entry == 64, filtered_here, none))
+    return jnp.sum(value, axis=1, keepdims=True)
 
 
 def is_any(value, choices):
@@ -207,7 +210,9 @@
 
 
 def substep_kernel(
-    plan,
+    target_hbm,
+    cutoff_hbm,
+    polar_hbm,
     tracer_hbm,
     zonal_hbm,
     merid_hbm,
@@ -218,6 +223,11 @@
     tw_hbm,
     next_out,
     slots_out,
+    target,
+    cutoff,
+    polar_rows,
+    plan_made,
+    plan,
     tracer,
     zonal,
     merid,
@@ -302,6 +312,9 @@
                 (inverse_hbm, inverse),
                 (within_hbm, within),
                 (tw_hbm, tw),
+                (target_hbm, target),
+                (cutoff_hbm, cutoff),
+                (polar_hbm, polar_rows),
             ]
         )
     ]
@@ -385,6 +398,11 @@
 
     for load in loads[4:]:
         load.wait()
+    lookup = routing_plan(target[...], cutoff[...], polar_rows[...], lon, lat)
+    plan_made[...] = jnp.broadcast_to(lookup, plan_made.shape)
+    plan_load = pltpu.make_async_copy(plan_made, plan, load_sem.at[11])
+    plan_load.start()
+    plan_load.wait()
 
     @pl.when(jnp.logical_or(is_worker, seam_worker))
     def _():
@@ -495,8 +513,8 @@
 
         def leave(k):
             to = lax.rem(place + 1 + k, PLACES)
-            outbound[2 * to] = by_row[plan[2 * to]]
-            outbound[2 * to + 1] = by_row[plan[2 * to + 1]]
+            outbound[2 * to] = by_row[plan[2 * to, 0]]
+            outbound[2 * to + 1] = by_row[plan[2 * to + 1, 0]]
             send(
                 outbound.at[pl.ds(2 * to, 2)],
                 column.at[source],
@@ -507,8 +525,8 @@
             ).start()
 
         each(PLACES - 1, leave)
-        column[source, 0] = by_row[plan[2 * place]]
-        column[source, 1] = by_row[plan[2 * place + 1]]
+        column[source, 0] = by_row[plan[2 * place, 0]]
+        column[source, 1] = by_row[plan[2 * place + 1, 0]]
 
     def pass_on(s):
         @pl.when(jnp.logical_not(jnp.logical_and(is_source, source == s)))
@@ -580,35 +598,40 @@
         sin_mid = jnp.concatenate([tw[1]] * (LEV // 2), axis=0)
         tables = (fh[...], fl[...], ih[...], il[...], wh[...], wl[...], cos_mid, sin_mid)
         values = with_edge_terms(gathered[...].reshape(N_LON * LEV, LANES))
-        smoothed[...] = band_filter(values, plan[64], tables).reshape(N_LON, LEV, LANES)
+        smoothed[...] = band_filter(values, plan[64, 0], tables).reshape(N_LON, LEV, LANES)
 
     @pl.when(is_worker)
     def _():
         @pl.when(across)
         def _():
-            each(
-                N_LON,
-                lambda k: send(
-                    smoothed.at[lax.rem(lon + k, N_LON)],
+            def far(k):
+                to = alternate(lon, k)
+                send(
+                    smoothed.at[to],
                     slot_in.at[half * SOURCES + work_source],
                     cross_send,
                     cross_recv,
-                    lax.rem(lon + k, N_LON),
+                    to,
                     lat_of(place, 1 - half),
-                ).start(),
-            )
-
-        each(
-            N_LON - 1,
-            lambda k: send(
-                smoothed.at[lax.rem(lon + 1 + k, N_LON)],
-                returned.at[work_source, work_half],
-                back_send,
-                back_recv.at[work_source],
-                lax.rem(lon + 1 + k, N_LON),
-                lat,
-            ).start(),
-        )
+                ).start()
+
+            each(N_LON, far)
+
+        def near(k):
+            to = inward(k)
+
+            @pl.when(to != lon)
+            def _():
+                send(
+                    smoothed.at[to],
+                    returned.at[work_source, work_half],
+                    back_send,
+                    back_recv.at[work_source],
+                    to,
+                    lat,
+                ).start()
+
+        each(N_LON, near)
         returned[work_source, work_half] = smoothed[lon]
 
     @pl.when(seam_worker)
@@ -701,7 +724,7 @@
             take(seam_slots[pair], seam_out_recv.at[pair])
 
     for slot in range(SLOTS):
-        slots_out[slot] = slot_in[plan[56 + slot]][:, :COLS]
+        slots_out[slot] = slot_in[plan[56 + slot, 0]][:, :COLS]
 
     @pl.when(is_source)
     def _():
@@ -709,7 +732,7 @@
         for j in range(ROWS):
             lat_row = lat * ROWS + j
             polar = jnp.logical_or(lat_row < NH, lat_row >= NLAT - NH)
-            filtered = homeward[plan[32 + j]][:, :COLS]
+            filtered = homeward[plan[32 + j, 0]][:, :COLS]
             next_out[:, j, :] = jnp.where(polar, tracer[:, j, :] + filtered, next_out[:, j, :])
 
     @pl.when(has_north)
@@ -770,7 +793,6 @@
 
 
 def shards(tracer, zonal_wind, meridional_wind, polar_target, cutoff_wave):
-    plan = routing_plan(polar_target, cutoff_wave)
     tables = [jnp.asarray(table) for table in filter_tables()]
     factors = jnp.asarray(row_factors())
     f32, bf16 = jnp.float32, jnp.bfloat16
@@ -779,15 +801,33 @@
     dma = pltpu.SemaphoreType.DMA
     square, wide = (LEV * N_LON, LEV * N_LON), (LANES, 2 * LANES)
     message = (LEV, LANES)
+    in_hbm = [
+        pltpu.with_memory_space_constraint(a, pltpu.HBM)
+        for a in (
+            polar_target.reshape(2, NPOLAR // 2),
+            cutoff_wave.reshape(2, NPOLAR // 2),
+            jnp.asarray(polar_row_table()),
+            tracer,
+            zonal_wind,
+            meridional_wind,
+            factors,
+            *tables,
+        )
+    ]
     return pl.pallas_call(
         substep_kernel,
         out_shape=(
             jax.ShapeDtypeStruct(block, f32),
             jax.ShapeDtypeStruct((SLOTS, LEV, COLS), f32),
         ),
-        in_specs=[pl.BlockSpec(memory_space=pltpu.SMEM)] + [anywhere] * 8,
+        in_specs=[anywhere] * 11,
         out_specs=(in_vmem, in_vmem),
         scratch_shapes=[
+            pltpu.VMEM((2, NPOLAR // 2), jnp.int32),
+            pltpu.VMEM((2, NPOLAR // 2), jnp.int32),
+            pltpu.VMEM((8, NPOLAR), jnp.int32),
+            pltpu.VMEM((ENTRIES, 128), jnp.int32),
+            pltpu.SMEM((ENTRIES, 128), jnp.int32),
             pltpu.VMEM(block, f32),
             pltpu.VMEM(block, f32),
             pltpu.VMEM(block, f32),
@@ -821,7 +861,7 @@
             pltpu.VMEM((N_LON, 2, *message), f32),
             pltpu.VMEM((N_LON, 2, *message), f32),
             pltpu.VMEM((2, *message), f32),
-            dma((8,)),
+            dma((12,)),
             dma((4,)),
             dma((4,)),
             dma,
@@ -842,10 +882,10 @@
             dma((2,)),
         ],
         compiler_params=pltpu.CompilerParams(
-            collective_id=0, has_side_effects=True, vmem_limit_bytes=60 * 2**20
+            collective_id=0, has_side_effects=True, vmem_limit_bytes=32 * 2**20
         ),
         name="substep",
-    )(plan, tracer, zonal_wind, meridional_wind, factors, *tables)
+    )(*in_hbm)
 
 
 def solution(mesh):

time: 83.1 us -> 74 us (0.89)
  the two profiles are of different devices: /device:TPU:6 before, /device:TPU:1 now
where the time goes in v4:
time: 74 us; the launch traced here: 72.7 us
  Pallas kernels  70.8 us (96%)
  local copies, waits for them, and re-layouts  1.31 us (2%)
    pallas_call x1, Pallas kernels, shards(): pl.pallas_call(substep_kernel, out_shape=(jax.ShapeDtypeStruct(block, f32...  70.8 us

profile of v4, /device:TPU:1, one launch (start us, length us, event | category | flops | bytes accessed | tf_op | source)
XLA Modules:
  0.0 72.7 jit_solution(3592372631812373200)
XLA Ops:
  0.6 70.8 %substep.1 = (f32[8,24,225]{2,1,0:T(8,128)S(1)}, f32[8,8,225]{2,1,0:T(8,128)S(1)}) custom-call(s32[2,128]{1,0:T(2,128)} %bitcast.2, s32[2,128]{1,0:T(2,128)} %bitcast.3, s32[8,256]{1,0:T(8,128)} %constant.17.clone.polar_hbm, f32[8,24,225]{2,1,0:T(8,128)} %tracer_hbm.1, f32[8,24,225]{2,1,0:T(8,128)} %zonal_hbm.1, f32[8,24,225]{2,1,0:T(8,128)} %merid_hbm.1, ...), custom_call_target="tpu_custom_call" | custom-call | tf_op jit(solution)/shard_map/substep/pallas_call | solution.py:817
  71.4 0.7 copy.15
  72.1 0.6 copy.16

commit v5 on v4

--- a/solution.py
+++ b/solution.py
@@ -17,8 +17,10 @@
 SOURCES, PLACES = 6, 16
 SEAM_LOW = (3, 27)
 SEAM_LON = 15
-WORKERS_FROM = 4
+SEAM_LINES = (3, 4, 27, 28)
+RELAYS = (10, 7, 24, 21)
 ENTRIES = 72
+NEAR = 4
 MESH = pl.DeviceIdType.MESH
 
 
@@ -39,13 +41,15 @@
 
 
 def worker_lon(worker):
-    return 2 * worker + WORKERS_FROM
+    return 2 * worker + jnp.where(worker < SOURCES, 2, 4)
 
 
 def worker_at(lon):
-    worker = lax.div(lon + 32 - WORKERS_FROM, 2) - 16
-    found = jnp.logical_and(lon >= WORKERS_FROM, lon < WORKERS_FROM + 4 * SOURCES)
-    return worker, jnp.logical_and(found, lax.rem(lon - WORKERS_FROM + 32, 2) == 0)
+    chip = lax.div(lon, 2)
+    worker = jnp.where(chip < SEAM_LON // 2, chip - 1, chip - 2)
+    found = jnp.logical_and(worker >= 0, worker < 2 * SOURCES)
+    found = jnp.logical_and(found, chip != SEAM_LON // 2)
+    return worker, jnp.logical_and(found, lax.rem(lon, 2) == 0)
 
 
 def alternate(lon, k):
@@ -134,6 +138,13 @@
     found = value == choices[0]
     for choice in choices[1:]:
         found = jnp.logical_or(found, value == choice)
+    return found
+
+
+def chosen(value, choices, results):
+    found = results[-1]
+    for choice, result in zip(choices[:-1], results[:-1]):
+        found = jnp.where(value == choice, result, found)
     return found
 
 
@@ -261,6 +272,7 @@
     seam_own,
     seam_other,
     seam_result,
+    far_in,
     load_sem,
     edge_send,
     edge_recv,
@@ -280,6 +292,12 @@
     seam_back_recv,
     seam_out_send,
     seam_out_recv,
+    line_sem,
+    bridge_sem,
+    both_sem,
+    seam_ready,
+    far_send,
+    far_recv,
 ):
     lon, lat = lax.axis_index("lon"), lax.axis_index("lat")
     half, place = half_of(lat), place_of(lat)
@@ -296,8 +314,24 @@
     seam_side = jnp.where(high_seam, 1, 0)
     other_lat = jnp.where(high_seam, lat - 1, lat + 1)
     seam_worker = jnp.logical_and(at_seam, lon == SEAM_LON)
-    has_north = jnp.logical_and(lat < N_LAT - 1, jnp.logical_not(low_seam))
-    has_south = jnp.logical_and(lat > 0, jnp.logical_not(high_seam))
+    has_north, has_south = lax.rem(lat, 4) != 3, lax.rem(lat, 4) != 0
+    far_north = jnp.logical_not(jnp.logical_or(has_north, jnp.logical_or(low_seam, lat == N_LAT - 1)))
+    far_south = jnp.logical_not(jnp.logical_or(has_south, jnp.logical_or(high_seam, lat == 0)))
+    any_north, any_south = jnp.logical_or(has_north, far_north), jnp.logical_or(has_south, far_south)
+    is_relay = is_any(lat, RELAYS)
+    served = chosen(lat, RELAYS, SEAM_LINES)
+    far_relay = chosen(other_lat, SEAM_LINES, RELAYS)
+    z = lax.div(lon, 2)
+    opposite = lat_of(place, 1 - half)
+    hands_north = jnp.logical_and(
+        lax.rem(lat, 4) == 3, jnp.logical_not(is_any(opposite, (*SEAM_LOW, N_LAT - 1)))
+    )
+    hands_south = jnp.logical_and(
+        lax.rem(lat, 4) == 0, jnp.logical_not(is_any(opposite, (0, *[low + 1 for low in SEAM_LOW])))
+    )
+    z_below, z_above = lax.max(z - NEAR, 0), lax.min(z + NEAR, N_LON // 2 - 1)
+    bridge = lon == jnp.where(half == 0, N_LON - 2, 0)
+    bridge_to = jnp.where(half == 0, 0, N_LON - 2)
     all_polar = jnp.logical_or(lat * ROWS + ROWS <= NH, lat * ROWS >= NLAT - NH)
 
     loads = [
@@ -328,32 +362,32 @@
             barrier, inc=1, device_id={"lon": to_lon, "lat": to_lat}, device_id_type=MESH
         )
 
-    @pl.when(has_north)
-    def _():
-        greet(lon, lat + 1)
-
-    @pl.when(has_south)
-    def _():
-        greet(lon, lat - 1)
-
-    each(N_LON, lambda k: greet(k, lat_of(place, 1 - half)))
-    each(N_LON - 1, lambda k: greet(lax.rem(lon + 1 + k, N_LON), lat))
-
-    @pl.when(is_source)
-    def _():
-        each(PLACES - 1, lambda k: greet(lon, lat_of(lax.rem(place + 1 + k, PLACES), half)))
-
-    @pl.when(jnp.logical_not(is_source))
-    def _():
-        each(SOURCES, lambda k: greet(lon, lat_of(source_place(k, half), half)))
+    each(PLACES - 1, lambda k: greet(lon, lat_of(lax.rem(place + 1 + k, PLACES), half)))
+
+    @pl.when(is_relay)
+    def _():
+        each(N_LON - 1, lambda k: greet(lax.rem(lon + 1 + k, N_LON), lat))
+
+    @pl.when(jnp.logical_not(is_relay))
+    def _():
+        def greet_near(k):
+            @pl.when(z_below * 2 + k != lon)
+            def _():
+                greet(z_below * 2 + k, lat)
+
+        each(2 * (z_above - z_below + 1), greet_near)
+
+    @pl.when(bridge)
+    def _():
+        greet(bridge_to, lat_of(place, 1 - half))
 
     @pl.when(at_seam)
     def _():
-        greet(SEAM_LON, other_lat)
+        greet(SEAM_LON, far_relay)
 
         @pl.when(seam_worker)
         def _():
-            each(N_LON, lambda k: greet(lax.rem(lon + k, N_LON), other_lat))
+            each(N_LON, lambda k: greet(lax.rem(lon + k, N_LON), far_relay))
 
     def send(what, where, send_sem, recv_sem, to_lon, to_lat):
         return pltpu.make_async_remote_copy(
@@ -412,13 +446,13 @@
 
     pl.semaphore_wait(
         barrier,
-        2 * N_LON
+        PLACES
         - 1
-        + jnp.where(is_source, PLACES - 1, SOURCES)
-        + jnp.where(has_north, 1, 0)
-        + jnp.where(has_south, 1, 0)
-        + jnp.where(at_seam, 1, 0)
-        + jnp.where(seam_worker, N_LON, 0),
+        + jnp.where(is_relay, N_LON - 1, 2 * (z_above - z_below) + 1)
+
+        + jnp.where(bridge, 1, 0)
+        + jnp.where(is_relay, 1, 0)
+        + jnp.where(jnp.logical_and(is_relay, lon == SEAM_LON), N_LON, 0),
     )
 
     @pl.when(has_north)
@@ -429,28 +463,39 @@
     def _():
         send(north_edge, north_in, edge_send.at[1], edge_recv.at[1], lon, lat - 1).start()
 
-    @pl.when(jnp.logical_not(all_polar))
-    def _():
-        send(lon_edge, west_in, edge_send.at[2], edge_recv.at[2], east, lat).start()
-        send(lon_edge, east_in, edge_send.at[3], edge_recv.at[3], west, lat).start()
-
-    @pl.when(low_seam)
-    def _():
-        send(
-            south_edge, seam_other.at[lon], seam_send.at[0], seam_recv.at[0], SEAM_LON, other_lat
-        ).start()
-
-    @pl.when(high_seam)
-    def _():
-        send(
-            north_edge, seam_other.at[lon, 0], seam_send.at[0], seam_recv.at[0], SEAM_LON, other_lat
-        ).start()
-
-    @pl.when(jnp.logical_not(has_south))
+    def tell(to_lon, to_lat, sem):
+        pl.semaphore_signal(
+            sem, inc=1, device_id={"lon": to_lon, "lat": to_lat}, device_id_type=MESH
+        )
+
+    def tell_along(distance, sem):
+        @pl.when(z >= distance)
+        def _():
+            tell(lon - 2 * distance, lat, sem)
+
+        @pl.when(z + distance < N_LON // 2)
+        def _():
+            tell(lon + 2 * distance, lat, sem)
+
+    def heard_along(distance, sem):
+        pl.semaphore_wait(
+            sem,
+            jnp.where(z >= distance, 1, 0) + jnp.where(z + distance < N_LON // 2, 1, 0),
+        )
+
+    @pl.when(is_relay)
+    def _():
+        tell(lon, served, seam_ready)
+
+    @pl.when(jnp.logical_not(is_relay))
+    def _():
+        tell_along(NEAR, line_sem.at[0])
+
+    @pl.when(jnp.logical_not(any_south))
     def _():
         south_in[...] = jnp.zeros(south_in.shape, jnp.float32)
 
-    @pl.when(jnp.logical_not(has_north))
+    @pl.when(jnp.logical_not(any_north))
     def _():
         north_in[...] = jnp.zeros(north_in.shape, jnp.float32)
 
@@ -459,11 +504,11 @@
         return jnp.broadcast_to(rows[None], (LEV, ROWS, LANES)).reshape(FLAT, LANES)
 
     def change_within():
-        @pl.when(has_south)
+        @pl.when(any_south)
         def _():
             take(south_in, edge_recv.at[0])
 
-        @pl.when(has_north)
+        @pl.when(any_north)
         def _():
             take(north_in, edge_recv.at[1])
 
@@ -499,17 +544,6 @@
         def _():
             seam_own[lon, 0] = by_row[0]
             seam_own[lon, 1] = north_edge[...]
-
-        @pl.when(jnp.logical_and(at_seam, lon != SEAM_LON))
-        def _():
-            send(
-                seam_own.at[lon],
-                seam_own.at[lon],
-                seam_send.at[1],
-                seam_recv.at[1],
-                SEAM_LON,
-                lat,
-            ).start()
 
         def leave(k):
             to = lax.rem(place + 1 + k, PLACES)
@@ -528,6 +562,53 @@
         column[source, 0] = by_row[plan[2 * place, 0]]
         column[source, 1] = by_row[plan[2 * place + 1, 0]]
 
+    @pl.when(jnp.logical_not(is_relay))
+    def _():
+        heard_along(NEAR, line_sem.at[0])
+        tell_along(2 * NEAR, line_sem.at[1])
+
+    @pl.when(at_seam)
+    def _():
+        pl.semaphore_wait(seam_ready, 1)
+
+    @pl.when(low_seam)
+    def _():
+        send(
+            south_edge, seam_other.at[lon], seam_send.at[0], seam_recv.at[0], SEAM_LON, other_lat
+        ).start()
+
+    @pl.when(high_seam)
+    def _():
+        send(
+            north_edge, seam_other.at[lon, 0], seam_send.at[0], seam_recv.at[0], SEAM_LON, other_lat
+        ).start()
+
+    @pl.when(jnp.logical_not(is_relay))
+    def _():
+        heard_along(2 * NEAR, line_sem.at[1])
+
+    @pl.when(jnp.logical_and(at_seam, lon != SEAM_LON))
+    def _():
+        send(
+            seam_own.at[lon],
+            seam_own.at[lon],
+            seam_send.at[1],
+            seam_recv.at[1],
+            SEAM_LON,
+            lat,
+        ).start()
+
+    @pl.when(bridge)
+    def _():
+        tell(bridge_to, lat_of(place, 1 - half), bridge_sem)
+        pl.semaphore_wait(bridge_sem, 1)
+        each(N_LON - 1, lambda k: tell(lax.rem(lon + 1 + k, N_LON), lat, both_sem))
+
+    @pl.when(jnp.logical_not(all_polar))
+    def _():
+        send(lon_edge, west_in, edge_send.at[2], edge_recv.at[2], east, lat).start()
+        send(lon_edge, east_in, edge_send.at[3], edge_recv.at[3], west, lat).start()
+
     def pass_on(s):
         @pl.when(jnp.logical_not(jnp.logical_and(is_source, source == s)))
         def _():
@@ -547,6 +628,105 @@
                 gathered[lon] = column[s, t_half]
 
     each(SOURCES, pass_on)
+
+    @pl.when(seam_worker)
+    def _():
+        take(seam_own.at[pl.ds(0, N_LON - 1)], seam_recv.at[1])
+
+        @pl.when(low_seam)
+        def _():
+            take(seam_other.at[pl.ds(0, N_LON // 2)], seam_recv.at[0])
+            scale = -0.5 * courant_number * factor[0, ROWS - 1 :, :] / factor[2, ROWS - 1 :, :]
+            scale = jnp.concatenate([scale, scale], axis=1)[None]
+            gathered[...] = seam_own[:, 0] + scale * seam_own[:, 1] * seam_other[:, 0]
+
+        @pl.when(high_seam)
+        def _():
+            take(seam_other, seam_recv.at[0])
+            scale = 0.5 * courant_number * factor[1, :1, :] / factor[2, :1, :]
+            scale = jnp.concatenate([scale, scale], axis=1)[None]
+            gathered[...] = seam_own[:, 0] + scale * seam_other[:, 1] * (
+                seam_other[:, 0] + seam_own[:, 1]
+            )
+
+    @pl.when(is_worker)
+    def _():
+        take(gathered.at[pl.ds(0, N_LON - 1)], gather_recv)
+
+    @pl.when(jnp.logical_or(is_worker, seam_worker))
+    def _():
+        cos_mid = jnp.concatenate([tw[0]] * (LEV // 2), axis=0)
+        sin_mid = jnp.concatenate([tw[1]] * (LEV // 2), axis=0)
+        tables = (fh[...], fl[...], ih[...], il[...], wh[...], wl[...], cos_mid, sin_mid)
+        values = with_edge_terms(gathered[...].reshape(N_LON * LEV, LANES))
+        smoothed[...] = band_filter(values, plan[64, 0], tables).reshape(N_LON, LEV, LANES)
+
+    @pl.when(jnp.logical_not(bridge))
+    def _():
+        pl.semaphore_wait(both_sem, 1)
+
+    @pl.when(far_north)
+    def _():
+        send(south_edge, far_in, edge_send.at[0], far_recv, lon, opposite).start()
+
+    @pl.when(far_south)
+    def _():
+        send(north_edge, far_in.at[0], edge_send.at[1], far_recv, lon, opposite).start()
+
+    @pl.when(is_worker)
+    def _():
+        @pl.when(across)
+        def _():
+            def far(k):
+                to = alternate(lon, k)
+                send(
+                    smoothed.at[to],
+                    slot_in.at[half * SOURCES + work_source],
+                    cross_send,
+                    cross_recv,
+                    to,
+                    lat_of(place, 1 - half),
+                ).start()
+
+            each(N_LON, far)
+
+        def near(k):
+            to = inward(k)
+
+            @pl.when(to != lon)
+            def _():
+                send(
+                    smoothed.at[to],
+                    returned.at[work_source, work_half],
+                    back_send,
+                    back_recv.at[work_source],
+                    to,
+                    lat,
+                ).start()
+
+        each(N_LON, near)
+        returned[work_source, work_half] = smoothed[lon]
+
+    @pl.when(seam_worker)
+    def _():
+        def to_seam(to, to_lat, sem):
+            send(
+                smoothed.at[to], seam_result.at[seam_side], sem, seam_back_recv, to, to_lat
+            ).start()
+
+        each(N_LON, lambda k: to_seam(alternate(lon, k), other_lat, seam_back_send.at[0]))
+        each(N_LON - 1, lambda k: to_seam(alternate(lon, k + 1), lat, seam_back_send.at[1]))
+        seam_result[seam_side] = smoothed[lon]
+
+    @pl.when(hands_north)
+    def _():
+        take(far_in, far_recv)
+        send(far_in, south_in, far_send, edge_recv.at[0], lon, opposite + 1).start()
+
+    @pl.when(hands_south)
+    def _():
+        take(far_in.at[0], far_recv)
+        send(far_in.at[0], north_in, far_send, edge_recv.at[1], lon, opposite - 1).start()
 
     @pl.when(jnp.logical_not(is_source))
     def _():
@@ -568,98 +748,6 @@
         change = jnp.where(lane == 0, change + half_courant * (wind_west * (tracer_west + t)), change)
         next_out[...] = (t + change).reshape(LEV, ROWS, LANES)[:, :, :COLS]
 
-    @pl.when(seam_worker)
-    def _():
-        take(seam_own.at[pl.ds(0, N_LON - 1)], seam_recv.at[1])
-
-        @pl.when(low_seam)
-        def _():
-            take(seam_other.at[pl.ds(0, N_LON // 2)], seam_recv.at[0])
-            scale = -0.5 * courant_number * factor[0, ROWS - 1 :, :] / factor[2, ROWS - 1 :, :]
-            scale = jnp.concatenate([scale, scale], axis=1)[None]
-            gathered[...] = seam_own[:, 0] + scale * seam_own[:, 1] * seam_other[:, 0]
-
-        @pl.when(high_seam)
-        def _():
-            take(seam_other, seam_recv.at[0])
-            scale = 0.5 * courant_number * factor[1, :1, :] / factor[2, :1, :]
-            scale = jnp.concatenate([scale, scale], axis=1)[None]
-            gathered[...] = seam_own[:, 0] + scale * seam_other[:, 1] * (
-                seam_other[:, 0] + seam_own[:, 1]
-            )
-
-    @pl.when(is_worker)
-    def _():
-        take(gathered.at[pl.ds(0, N_LON - 1)], gather_recv)
-
-    @pl.when(jnp.logical_or(is_worker, seam_worker))
-    def _():
-        cos_mid = jnp.concatenate([tw[0]] * (LEV // 2), axis=0)
-        sin_mid = jnp.concatenate([tw[1]] * (LEV // 2), axis=0)
-        tables = (fh[...], fl[...], ih[...], il[...], wh[...], wl[...], cos_mid, sin_mid)
-        values = with_edge_terms(gathered[...].reshape(N_LON * LEV, LANES))
-        smoothed[...] = band_filter(values, plan[64, 0], tables).reshape(N_LON, LEV, LANES)
-
-    @pl.when(is_worker)
-    def _():
-        @pl.when(across)
-        def _():
-            def far(k):
-                to = alternate(lon, k)
-                send(
-                    smoothed.at[to],
-                    slot_in.at[half * SOURCES + work_source],
-                    cross_send,
-                    cross_recv,
-                    to,
-                    lat_of(place, 1 - half),
-                ).start()
-
-            each(N_LON, far)
-
-        def near(k):
-            to = inward(k)
-
-            @pl.when(to != lon)
-            def _():
-                send(
-                    smoothed.at[to],
-                    returned.at[work_source, work_half],
-                    back_send,
-                    back_recv.at[work_source],
-                    to,
-                    lat,
-                ).start()
-
-        each(N_LON, near)
-        returned[work_source, work_half] = smoothed[lon]
-
-    @pl.when(seam_worker)
-    def _():
-        each(
-            N_LON,
-            lambda k: send(
-                smoothed.at[lax.rem(lon + k, N_LON)],
-                seam_result.at[seam_side],
-                seam_back_send.at[0],
-                seam_back_recv,
-                lax.rem(lon + k, N_LON),
-                other_lat,
-            ).start(),
-        )
-        each(
-            N_LON - 1,
-            lambda k: send(
-                smoothed.at[lax.rem(lon + 1 + k, N_LON)],
-                seam_result.at[seam_side],
-                seam_back_send.at[1],
-                seam_back_recv,
-                lax.rem(lon + 1 + k, N_LON),
-                lat,
-            ).start(),
-        )
-        seam_result[seam_side] = smoothed[lon]
-
     seam_pair = jnp.where(lat < NLAT // ROWS // 2, 0, 1)
     seam_slots = [slot_in.at[pl.ds(2 * SOURCES + 2 * pair, 2)] for pair in range(2)]
 
@@ -735,11 +823,19 @@
             filtered = homeward[plan[32 + j, 0]][:, :COLS]
             next_out[:, j, :] = jnp.where(polar, tracer[:, j, :] + filtered, next_out[:, j, :])
 
-    @pl.when(has_north)
+    @pl.when(hands_north)
+    def _():
+        sent(far_in, far_send)
+
+    @pl.when(hands_south)
+    def _():
+        sent(far_in.at[0], far_send)
+
+    @pl.when(any_north)
     def _():
         sent(south_edge, edge_send.at[0])
 
-    @pl.when(has_south)
+    @pl.when(any_south)
     def _():
         sent(north_edge, edge_send.at[1])
 
@@ -861,6 +957,7 @@
             pltpu.VMEM((N_LON, 2, *message), f32),
             pltpu.VMEM((N_LON, 2, *message), f32),
             pltpu.VMEM((2, *message), f32),
+            pltpu.VMEM((2, *message), f32),
             dma((12,)),
             dma((4,)),
             dma((4,)),
@@ -880,6 +977,12 @@
             dma,
             dma,
             dma((2,)),
+            pltpu.SemaphoreType.REGULAR((2,)),
+            pltpu.SemaphoreType.REGULAR,
+            pltpu.SemaphoreType.REGULAR,
+            pltpu.SemaphoreType.REGULAR,
+            dma,
+            dma,
         ],
         compiler_params=pltpu.CompilerParams(
             collective_id=0, has_side_effects=True, vmem_limit_bytes=32 * 2**20

time: 74 us -> 69.8 us (0.943)
  Pallas kernels: 70.8 us -> 67.3 us
    pallas_call x1, Pallas kernels: 70.8 us -> 67.3 us  [shards(): pl.pallas_call(substep_kernel, out_shape=(jax.ShapeDtypeStruct(block, f32...]
where the time goes in v5:
time: 69.8 us; the launch traced here: 69.3 us
  Pallas kernels  67.3 us (96%)
  local copies, waits for them, and re-layouts  1.31 us (2%)
    pallas_call x1, Pallas kernels, shards(): pl.pallas_call(substep_kernel, out_shape=(jax.ShapeDtypeStruct(block, f32...  67.3 us

profile of v5, /device:TPU:1, one launch (start us, length us, event | category | flops | bytes accessed | tf_op | source)
XLA Modules:
  0.0 69.3 jit_solution(2025496203634144662)
XLA Ops:
  0.6 67.3 %substep.1 = (f32[8,24,225]{2,1,0:T(8,128)S(1)}, f32[8,8,225]{2,1,0:T(8,128)S(1)}) custom-call(s32[2,128]{1,0:T(2,128)} %bitcast.2, s32[2,128]{1,0:T(2,128)} %bitcast.3, s32[8,256]{1,0:T(8,128)} %constant.17.clone.polar_hbm, f32[8,24,225]{2,1,0:T(8,128)} %tracer_hbm.1, f32[8,24,225]{2,1,0:T(8,128)} %zonal_hbm.1, f32[8,24,225]{2,1,0:T(8,128)} %merid_hbm.1, ...), custom_call_target="tpu_custom_call" | custom-call | tf_op jit(solution)/shard_map/substep/pallas_call | solution.py:913
  68.0 0.7 copy.15
  68.7 0.6 copy.16

commit v6 on v5

--- a/solution.py
+++ b/solution.py
@@ -55,11 +55,6 @@
 def alternate(lon, k):
     step = lax.div(k + 1, 2)
     return lax.rem(lon + N_LON + jnp.where(lax.rem(k, 2) == 1, step, -step), N_LON)
-
-
-def inward(k):
-    step = lax.div(k, 2)
-    return jnp.where(lax.rem(k, 2) == 1, N_LON - 1 - step, step)
 
 
 def filter_tables():
@@ -524,216 +519,7 @@
         change = -courant_number * (zonal_div + (north_flux - south_flux) / by_lane(2))
         return t, u, jnp.where(lane < COLS, change, 0.0), lane
 
-    @pl.when(is_source)
-    def _():
-        t, u, change, lane = change_within()
-        increment[...] = change
-        last_wind = 0.5 * courant_number * u[:, COLS - 1 : COLS]
-        marked = jnp.where(lane == COLS, t[:, 0:1], change)
-        marked = jnp.where(lane == COLS + 1, last_wind, marked)
-        marked = jnp.where(lane == COLS + 2, last_wind * t[:, COLS - 1 : COLS], marked)
-        for level in range(LEV):
-            by_row[:, level, :] = marked[level * ROWS : (level + 1) * ROWS, :]
-
-        @pl.when(low_seam)
-        def _():
-            seam_own[lon, 0] = by_row[ROWS - 1]
-            seam_own[lon, 1] = south_edge[1]
-
-        @pl.when(high_seam)
-        def _():
-            seam_own[lon, 0] = by_row[0]
-            seam_own[lon, 1] = north_edge[...]
-
-        def leave(k):
-            to = lax.rem(place + 1 + k, PLACES)
-            outbound[2 * to] = by_row[plan[2 * to, 0]]
-            outbound[2 * to + 1] = by_row[plan[2 * to + 1, 0]]
-            send(
-                outbound.at[pl.ds(2 * to, 2)],
-                column.at[source],
-                out_send,
-                out_recv.at[source],
-                lon,
-                lat_of(to, half),
-            ).start()
-
-        each(PLACES - 1, leave)
-        column[source, 0] = by_row[plan[2 * place, 0]]
-        column[source, 1] = by_row[plan[2 * place + 1, 0]]
-
-    @pl.when(jnp.logical_not(is_relay))
-    def _():
-        heard_along(NEAR, line_sem.at[0])
-        tell_along(2 * NEAR, line_sem.at[1])
-
-    @pl.when(at_seam)
-    def _():
-        pl.semaphore_wait(seam_ready, 1)
-
-    @pl.when(low_seam)
-    def _():
-        send(
-            south_edge, seam_other.at[lon], seam_send.at[0], seam_recv.at[0], SEAM_LON, other_lat
-        ).start()
-
-    @pl.when(high_seam)
-    def _():
-        send(
-            north_edge, seam_other.at[lon, 0], seam_send.at[0], seam_recv.at[0], SEAM_LON, other_lat
-        ).start()
-
-    @pl.when(jnp.logical_not(is_relay))
-    def _():
-        heard_along(2 * NEAR, line_sem.at[1])
-
-    @pl.when(jnp.logical_and(at_seam, lon != SEAM_LON))
-    def _():
-        send(
-            seam_own.at[lon],
-            seam_own.at[lon],
-            seam_send.at[1],
-            seam_recv.at[1],
-            SEAM_LON,
-            lat,
-        ).start()
-
-    @pl.when(bridge)
-    def _():
-        tell(bridge_to, lat_of(place, 1 - half), bridge_sem)
-        pl.semaphore_wait(bridge_sem, 1)
-        each(N_LON - 1, lambda k: tell(lax.rem(lon + 1 + k, N_LON), lat, both_sem))
-
-    @pl.when(jnp.logical_not(all_polar))
-    def _():
-        send(lon_edge, west_in, edge_send.at[2], edge_recv.at[2], east, lat).start()
-        send(lon_edge, east_in, edge_send.at[3], edge_recv.at[3], west, lat).start()
-
-    def pass_on(s):
-        @pl.when(jnp.logical_not(jnp.logical_and(is_source, source == s)))
-        def _():
-            take(column.at[s], out_recv.at[s])
-
-        for t_half in range(2):
-            to = worker_lon(2 * s + t_half)
-
-            @pl.when(to != lon)
-            def _():
-                send(
-                    column.at[s, t_half], gathered.at[lon], gather_send, gather_recv, to, lat
-                ).start()
-
-            @pl.when(to == lon)
-            def _():
-                gathered[lon] = column[s, t_half]
-
-    each(SOURCES, pass_on)
-
-    @pl.when(seam_worker)
-    def _():
-        take(seam_own.at[pl.ds(0, N_LON - 1)], seam_recv.at[1])
-
-        @pl.when(low_seam)
-        def _():
-            take(seam_other.at[pl.ds(0, N_LON // 2)], seam_recv.at[0])
-            scale = -0.5 * courant_number * factor[0, ROWS - 1 :, :] / factor[2, ROWS - 1 :, :]
-            scale = jnp.concatenate([scale, scale], axis=1)[None]
-            gathered[...] = seam_own[:, 0] + scale * seam_own[:, 1] * seam_other[:, 0]
-
-        @pl.when(high_seam)
-        def _():
-            take(seam_other, seam_recv.at[0])
-            scale = 0.5 * courant_number * factor[1, :1, :] / factor[2, :1, :]
-            scale = jnp.concatenate([scale, scale], axis=1)[None]
-            gathered[...] = seam_own[:, 0] + scale * seam_other[:, 1] * (
-                seam_other[:, 0] + seam_own[:, 1]
-            )
-
-    @pl.when(is_worker)
-    def _():
-        take(gathered.at[pl.ds(0, N_LON - 1)], gather_recv)
-
-    @pl.when(jnp.logical_or(is_worker, seam_worker))
-    def _():
-        cos_mid = jnp.concatenate([tw[0]] * (LEV // 2), axis=0)
-        sin_mid = jnp.concatenate([tw[1]] * (LEV // 2), axis=0)
-        tables = (fh[...], fl[...], ih[...], il[...], wh[...], wl[...], cos_mid, sin_mid)
-        values = with_edge_terms(gathered[...].reshape(N_LON * LEV, LANES))
-        smoothed[...] = band_filter(values, plan[64, 0], tables).reshape(N_LON, LEV, LANES)
-
-    @pl.when(jnp.logical_not(bridge))
-    def _():
-        pl.semaphore_wait(both_sem, 1)
-
-    @pl.when(far_north)
-    def _():
-        send(south_edge, far_in, edge_send.at[0], far_recv, lon, opposite).start()
-
-    @pl.when(far_south)
-    def _():
-        send(north_edge, far_in.at[0], edge_send.at[1], far_recv, lon, opposite).start()
-
-    @pl.when(is_worker)
-    def _():
-        @pl.when(across)
-        def _():
-            def far(k):
-                to = alternate(lon, k)
-                send(
-                    smoothed.at[to],
-                    slot_in.at[half * SOURCES + work_source],
-                    cross_send,
-                    cross_recv,
-                    to,
-                    lat_of(place, 1 - half),
-                ).start()
-
-            each(N_LON, far)
-
-        def near(k):
-            to = inward(k)
-
-            @pl.when(to != lon)
-            def _():
-                send(
-                    smoothed.at[to],
-                    returned.at[work_source, work_half],
-                    back_send,
-                    back_recv.at[work_source],
-                    to,
-                    lat,
-                ).start()
-
-        each(N_LON, near)
-        returned[work_source, work_half] = smoothed[lon]
-
-    @pl.when(seam_worker)
-    def _():
-        def to_seam(to, to_lat, sem):
-            send(
-                smoothed.at[to], seam_result.at[seam_side], sem, seam_back_recv, to, to_lat
-            ).start()
-
-        each(N_LON, lambda k: to_seam(alternate(lon, k), other_lat, seam_back_send.at[0]))
-        each(N_LON - 1, lambda k: to_seam(alternate(lon, k + 1), lat, seam_back_send.at[1]))
-        seam_result[seam_side] = smoothed[lon]
-
-    @pl.when(hands_north)
-    def _():
-        take(far_in, far_recv)
-        send(far_in, south_in, far_send, edge_recv.at[0], lon, opposite + 1).start()
-
-    @pl.when(hands_south)
-    def _():
-        take(far_in.at[0], far_recv)
-        send(far_in.at[0], north_in, far_send, edge_recv.at[1], lon, opposite - 1).start()
-
-    @pl.when(jnp.logical_not(is_source))
-    def _():
-        increment[...] = change_within()[2]
-
-    @pl.when(jnp.logical_not(all_polar))
-    def _():
+    def plain_rows():
         take(west_in, edge_recv.at[2])
         take(east_in, edge_recv.at[3])
         columns = jnp.concatenate(
@@ -748,6 +534,239 @@
         change = jnp.where(lane == 0, change + half_courant * (wind_west * (tracer_west + t)), change)
         next_out[...] = (t + change).reshape(LEV, ROWS, LANES)[:, :, :COLS]
 
+    @pl.when(is_source)
+    def _():
+        t, u, change, lane = change_within()
+        increment[...] = change
+        last_wind = 0.5 * courant_number * u[:, COLS - 1 : COLS]
+        marked = jnp.where(lane == COLS, t[:, 0:1], change)
+        marked = jnp.where(lane == COLS + 1, last_wind, marked)
+        marked = jnp.where(lane == COLS + 2, last_wind * t[:, COLS - 1 : COLS], marked)
+        for level in range(LEV):
+            by_row[:, level, :] = marked[level * ROWS : (level + 1) * ROWS, :]
+
+        @pl.when(low_seam)
+        def _():
+            seam_own[lon, 0] = by_row[ROWS - 1]
+            seam_own[lon, 1] = south_edge[1]
+
+        @pl.when(high_seam)
+        def _():
+            seam_own[lon, 0] = by_row[0]
+            seam_own[lon, 1] = north_edge[...]
+
+        def leave(k):
+            to = lax.rem(place + 1 + k, PLACES)
+            outbound[2 * to] = by_row[plan[2 * to, 0]]
+            outbound[2 * to + 1] = by_row[plan[2 * to + 1, 0]]
+            send(
+                outbound.at[pl.ds(2 * to, 2)],
+                column.at[source],
+                out_send,
+                out_recv.at[source],
+                lon,
+                lat_of(to, half),
+            ).start()
+
+        each(PLACES - 1, leave)
+        column[source, 0] = by_row[plan[2 * place, 0]]
+        column[source, 1] = by_row[plan[2 * place + 1, 0]]
+
+    @pl.when(jnp.logical_not(is_relay))
+    def _():
+        heard_along(NEAR, line_sem.at[0])
+        tell_along(2 * NEAR, line_sem.at[1])
+
+    @pl.when(at_seam)
+    def _():
+        pl.semaphore_wait(seam_ready, 1)
+
+    @pl.when(low_seam)
+    def _():
+        send(
+            south_edge, seam_other.at[lon], seam_send.at[0], seam_recv.at[0], SEAM_LON, other_lat
+        ).start()
+
+    @pl.when(high_seam)
+    def _():
+        send(
+            north_edge, seam_other.at[lon, 0], seam_send.at[0], seam_recv.at[0], SEAM_LON, other_lat
+        ).start()
+
+    @pl.when(jnp.logical_not(is_relay))
+    def _():
+        heard_along(2 * NEAR, line_sem.at[1])
+
+    @pl.when(jnp.logical_and(at_seam, lon != SEAM_LON))
+    def _():
+        send(
+            seam_own.at[lon],
+            seam_own.at[lon],
+            seam_send.at[1],
+            seam_recv.at[1],
+            SEAM_LON,
+            lat,
+        ).start()
+
+    @pl.when(bridge)
+    def _():
+        tell(bridge_to, lat_of(place, 1 - half), bridge_sem)
+        pl.semaphore_wait(bridge_sem, 1)
+        each(N_LON - 1, lambda k: tell(lax.rem(lon + 1 + k, N_LON), lat, both_sem))
+
+    @pl.when(jnp.logical_not(all_polar))
+    def _():
+        send(lon_edge, west_in, edge_send.at[2], edge_recv.at[2], east, lat).start()
+        send(lon_edge, east_in, edge_send.at[3], edge_recv.at[3], west, lat).start()
+
+    def to_worker(s, t_half):
+        to = worker_lon(2 * s + t_half)
+
+        @pl.when(to != lon)
+        def _():
+            send(
+                column.at[s, t_half], gathered.at[lon], gather_send, gather_recv, to, lat
+            ).start()
+
+        @pl.when(to == lon)
+        def _():
+            gathered[lon] = column[s, t_half]
+
+    def pass_on(s):
+        @pl.when(jnp.logical_not(jnp.logical_and(is_source, source == s)))
+        def _():
+            take(column.at[s], out_recv.at[s])
+
+        to_worker(s, 0)
+
+        @pl.when(half == 0)
+        def _():
+            to_worker(s, 1)
+
+    each(SOURCES, pass_on)
+
+    @pl.when(half == 1)
+    def _():
+        each(SOURCES, lambda s: to_worker(s, 1))
+
+    @pl.when(jnp.logical_not(bridge))
+    def _():
+        pl.semaphore_wait(both_sem, 1)
+
+    @pl.when(far_north)
+    def _():
+        send(south_edge, far_in, edge_send.at[0], far_recv, lon, opposite).start()
+
+    @pl.when(far_south)
+    def _():
+        send(north_edge, far_in.at[0], edge_send.at[1], far_recv, lon, opposite).start()
+
+    @pl.when(seam_worker)
+    def _():
+        take(seam_own.at[pl.ds(0, N_LON - 1)], seam_recv.at[1])
+
+        @pl.when(low_seam)
+        def _():
+            take(seam_other.at[pl.ds(0, N_LON // 2)], seam_recv.at[0])
+            scale = -0.5 * courant_number * factor[0, ROWS - 1 :, :] / factor[2, ROWS - 1 :, :]
+            scale = jnp.concatenate([scale, scale], axis=1)[None]
+            gathered[...] = seam_own[:, 0] + scale * seam_own[:, 1] * seam_other[:, 0]
+
+        @pl.when(high_seam)
+        def _():
+            take(seam_other, seam_recv.at[0])
+            scale = 0.5 * courant_number * factor[1, :1, :] / factor[2, :1, :]
+            scale = jnp.concatenate([scale, scale], axis=1)[None]
+            gathered[...] = seam_own[:, 0] + scale * seam_other[:, 1] * (
+                seam_other[:, 0] + seam_own[:, 1]
+            )
+
+    @pl.when(is_worker)
+    def _():
+        take(gathered.at[pl.ds(0, N_LON - 1)], gather_recv)
+
+    @pl.when(jnp.logical_or(is_worker, seam_worker))
+    def _():
+        cos_mid = jnp.concatenate([tw[0]] * (LEV // 2), axis=0)
+        sin_mid = jnp.concatenate([tw[1]] * (LEV // 2), axis=0)
+        tables = (fh[...], fl[...], ih[...], il[...], wh[...], wl[...], cos_mid, sin_mid)
+        values = with_edge_terms(gathered[...].reshape(N_LON * LEV, LANES))
+        smoothed[...] = band_filter(values, plan[64, 0], tables).reshape(N_LON, LEV, LANES)
+
+    @pl.when(is_worker)
+    def _():
+        def to_slot(to):
+            send(
+                smoothed.at[to],
+                slot_in.at[half * SOURCES + work_source],
+                cross_send,
+                cross_recv,
+                to,
+                opposite,
+            ).start()
+
+        def to_line(to):
+            @pl.when(to != lon)
+            def _():
+                send(
+                    smoothed.at[to],
+                    returned.at[work_source, work_half],
+                    back_send,
+                    back_recv.at[work_source],
+                    to,
+                    lat,
+                ).start()
+
+        @pl.when(jnp.logical_and(across, half == 1))
+        def _():
+            each(N_LON, to_slot)
+
+        each(N_LON, to_line)
+
+        @pl.when(jnp.logical_and(across, half == 0))
+        def _():
+            each(N_LON, lambda k: to_slot(alternate(lon, k)))
+
+        returned[work_source, work_half] = smoothed[lon]
+
+    @pl.when(seam_worker)
+    def _():
+        def to_seam(to, to_lat, sem):
+            send(
+                smoothed.at[to], seam_result.at[seam_side], sem, seam_back_recv, to, to_lat
+            ).start()
+
+        def to_own_line(to):
+            @pl.when(to != lon)
+            def _():
+                to_seam(to, lat, seam_back_send.at[1])
+
+        @pl.when(half == 0)
+        def _():
+            each(N_LON, to_own_line)
+
+        each(N_LON, lambda to: to_seam(to, other_lat, seam_back_send.at[0]))
+
+        @pl.when(half == 1)
+        def _():
+            each(N_LON, to_own_line)
+
+        seam_result[seam_side] = smoothed[lon]
+
+    @pl.when(hands_north)
+    def _():
+        take(far_in, far_recv)
+        send(far_in, south_in, far_send, edge_recv.at[0], lon, opposite + 1).start()
+
+    @pl.when(hands_south)
+    def _():
+        take(far_in.at[0], far_recv)
+        send(far_in.at[0], north_in, far_send, edge_recv.at[1], lon, opposite - 1).start()
+
+    @pl.when(jnp.logical_and(is_source, jnp.logical_not(all_polar)))
+    def _():
+        plain_rows()
+
     seam_pair = jnp.where(lat < NLAT // ROWS // 2, 0, 1)
     seam_slots = [slot_in.at[pl.ds(2 * SOURCES + 2 * pair, 2)] for pair in range(2)]
 
@@ -813,6 +832,11 @@
 
     for slot in range(SLOTS):
         slots_out[slot] = slot_in[plan[56 + slot, 0]][:, :COLS]
+
+    @pl.when(jnp.logical_not(is_source))
+    def _():
+        increment[...] = change_within()[2]
+        plain_rows()
 
     @pl.when(is_source)
     def _():

time: 69.8 us -> 65.3 us (0.936)
  the two profiles are of different devices: /device:TPU:1 before, /device:TPU:290 now
where the time goes in v6:
time: 65.3 us; the launch traced here: 65.1 us
  Pallas kernels  63.1 us (97%)
  local copies, waits for them, and re-layouts  1.31 us (2%)
    pallas_call x1, Pallas kernels, shards(): pl.pallas_call(substep_kernel, out_shape=(jax.ShapeDtypeStruct(block, f32...  63.1 us
    unnamed x2, local copies, waits for them, and re-layouts  1.31 us

profile of v6, /device:TPU:290, one launch (start us, length us, event | category | flops | bytes accessed | tf_op | source)
XLA Modules:
  0.0 65.1 jit_solution(982776358850161935)
XLA Ops:
  0.6 63.1 %substep.1 = (f32[8,24,225]{2,1,0:T(8,128)S(1)}, f32[8,8,225]{2,1,0:T(8,128)S(1)}) custom-call(s32[2,128]{1,0:T(2,128)} %bitcast.2, s32[2,128]{1,0:T(2,128)} %bitcast.3, s32[8,256]{1,0:T(8,128)} %constant.17.clone.polar_hbm, f32[8,24,225]{2,1,0:T(8,128)} %tracer_hbm.1, f32[8,24,225]{2,1,0:T(8,128)} %zonal_hbm.1, f32[8,24,225]{2,1,0:T(8,128)} %merid_hbm.1, ...), custom_call_target="tpu_custom_call" | custom-call | tf_op jit(solution)/shard_map/substep/pallas_call | solution.py:937
  63.8 0.7 %copy.15 = f32[8,24,225]{2,1,0:T(8,128)} copy(f32[8,24,225]{2,1,0:T(8,128)S(1)} %get-tuple-element.4) | data formatting | bytes 345600
  64.5 0.6 copy.16

commit v7 on v6

--- a/solution.py
+++ b/solution.py
@@ -17,6 +17,7 @@
 SOURCES, PLACES = 6, 16
 SEAM_LOW = (3, 27)
 SEAM_LON = 15
+LATE_SEAM_LON = 21
 SEAM_LINES = (3, 4, 27, 28)
 RELAYS = (10, 7, 24, 21)
 ENTRIES = 72
@@ -209,10 +210,6 @@
 def widened(block):
     pad = jnp.zeros((LEV, ROWS, LANES - COLS), jnp.float32)
     return jnp.concatenate([block, pad], axis=2).reshape(FLAT, LANES)
-
-
-def spread_rows(edge):
-    return jnp.broadcast_to(edge[:, None, :], (LEV, ROWS, LANES)).reshape(FLAT, LANES)
 
 
 def substep_kernel(
@@ -303,12 +300,14 @@
     work_source, work_half = lax.div(worker, 2), lax.rem(worker, 2)
     across = jnp.logical_and(is_worker, work_half != half)
     east, west = lax.rem(lon + 1, N_LON), lax.rem(lon + N_LON - 1, N_LON)
+    own_seam_lon = jnp.where(half == 0, SEAM_LON, LATE_SEAM_LON)
+    other_seam_lon = jnp.where(half == 0, LATE_SEAM_LON, SEAM_LON)
     low_seam = is_any(lat, SEAM_LOW)
     high_seam = is_any(lat, [low + 1 for low in SEAM_LOW])
     at_seam = jnp.logical_or(low_seam, high_seam)
     seam_side = jnp.where(high_seam, 1, 0)
     other_lat = jnp.where(high_seam, lat - 1, lat + 1)
-    seam_worker = jnp.logical_and(at_seam, lon == SEAM_LON)
+    seam_worker = jnp.logical_and(at_seam, lon == own_seam_lon)
     has_north, has_south = lax.rem(lat, 4) != 3, lax.rem(lat, 4) != 0
     far_north = jnp.logical_not(jnp.logical_or(has_north, jnp.logical_or(low_seam, lat == N_LAT - 1)))
     far_south = jnp.logical_not(jnp.logical_or(has_south, jnp.logical_or(high_seam, lat == 0)))
@@ -378,7 +377,7 @@
 
     @pl.when(at_seam)
     def _():
-        greet(SEAM_LON, far_relay)
+        greet(other_seam_lon, far_relay)
 
         @pl.when(seam_worker)
         def _():
@@ -425,6 +424,29 @@
         south_edge[1, level : level + 1, :] = v[top : top + 1]
         north_edge[level : level + 1, :] = t[bottom : bottom + 1]
 
+    def by_lane(i):
+        rows = jnp.concatenate([factor[i], factor[i]], axis=1)
+        return jnp.broadcast_to(rows[None], (LEV, ROWS, LANES)).reshape(FLAT, LANES)
+
+    row = lax.rem(lax.broadcasted_iota(jnp.int32, (FLAT, LANES), 0), ROWS)
+    east_flux = u * (t + pltpu.roll(t, LANES - 1, 1)) * 0.5
+    zonal_div = east_flux - pltpu.roll(east_flux, 1, 1)
+    above = jnp.where(row == ROWS - 1, 0.0, pltpu.roll(t, FLAT - 1, 0))
+    north_flux = v * by_lane(0) * (t + above) * 0.5
+    south_flux = jnp.where(row == 0, 0.0, pltpu.roll(north_flux, 1, 0))
+    change = -courant_number * (zonal_div + (north_flux - south_flux) / by_lane(2))
+    change = jnp.where(lane < COLS, change, 0.0)
+    increment[...] = change
+
+    @pl.when(is_source)
+    def _():
+        last_wind = 0.5 * courant_number * u[:, COLS - 1 : COLS]
+        marked = jnp.where(lane == COLS, t[:, 0:1], change)
+        marked = jnp.where(lane == COLS + 1, last_wind, marked)
+        marked = jnp.where(lane == COLS + 2, last_wind * t[:, COLS - 1 : COLS], marked)
+        for level in range(LEV):
+            by_row[:, level, :] = marked[level * ROWS : (level + 1) * ROWS, :]
+
     for load in loads[4:]:
         load.wait()
     lookup = routing_plan(target[...], cutoff[...], polar_rows[...], lon, lat)
@@ -433,12 +455,6 @@
     plan_load.start()
     plan_load.wait()
 
-    @pl.when(jnp.logical_or(is_worker, seam_worker))
-    def _():
-        fh[...], fl[...] = split_value(forward[...])
-        ih[...], il[...] = split_value(inverse[...])
-        wh[...], wl[...] = split_value(within[...])
-
     pl.semaphore_wait(
         barrier,
         PLACES
@@ -447,7 +463,7 @@
 
         + jnp.where(bridge, 1, 0)
         + jnp.where(is_relay, 1, 0)
-        + jnp.where(jnp.logical_and(is_relay, lon == SEAM_LON), N_LON, 0),
+        + jnp.where(jnp.logical_and(is_relay, lon == own_seam_lon), N_LON, 0),
     )
 
     @pl.when(has_north)
@@ -486,40 +502,25 @@
     def _():
         tell_along(NEAR, line_sem.at[0])
 
-    @pl.when(jnp.logical_not(any_south))
-    def _():
-        south_in[...] = jnp.zeros(south_in.shape, jnp.float32)
-
-    @pl.when(jnp.logical_not(any_north))
-    def _():
-        north_in[...] = jnp.zeros(north_in.shape, jnp.float32)
-
-    def by_lane(i):
-        rows = jnp.concatenate([factor[i], factor[i]], axis=1)
-        return jnp.broadcast_to(rows[None], (LEV, ROWS, LANES)).reshape(FLAT, LANES)
-
-    def change_within():
-        @pl.when(any_south)
+    def edge_scale(face, row):
+        scale = 0.5 * courant_number * factor[face, row : row + 1, :] / factor[2, row : row + 1, :]
+        return jnp.concatenate([scale, scale], axis=1)
+
+    def from_north():
+        return -edge_scale(0, ROWS - 1) * south_edge[1] * north_in[...]
+
+    def from_south():
+        return edge_scale(1, 0) * south_in[1] * (south_in[0] + north_edge[...])
+
+    def plain_rows():
+        @pl.when(jnp.logical_and(any_south, jnp.logical_not(is_source)))
         def _():
             take(south_in, edge_recv.at[0])
 
-        @pl.when(any_north)
+        @pl.when(jnp.logical_and(any_north, jnp.logical_not(is_source)))
         def _():
             take(north_in, edge_recv.at[1])
 
-        t, u, v = widened(tracer[...]), widened(zonal[...]), widened(merid[...])
-        row = lax.rem(lax.broadcasted_iota(jnp.int32, (FLAT, LANES), 0), ROWS)
-        lane = lax.broadcasted_iota(jnp.int32, (FLAT, LANES), 1)
-        east_flux = u * (t + pltpu.roll(t, LANES - 1, 1)) * 0.5
-        zonal_div = east_flux - pltpu.roll(east_flux, 1, 1)
-        above = jnp.where(row == ROWS - 1, spread_rows(north_in[...]), pltpu.roll(t, FLAT - 1, 0))
-        north_flux = v * by_lane(0) * (t + above) * 0.5
-        below_flux = spread_rows(south_in[1]) * by_lane(1) * (spread_rows(south_in[0]) + t) * 0.5
-        south_flux = jnp.where(row == 0, below_flux, pltpu.roll(north_flux, 1, 0))
-        change = -courant_number * (zonal_div + (north_flux - south_flux) / by_lane(2))
-        return t, u, jnp.where(lane < COLS, change, 0.0), lane
-
-    def plain_rows():
         take(west_in, edge_recv.at[2])
         take(east_in, edge_recv.at[3])
         columns = jnp.concatenate(
@@ -534,16 +535,25 @@
         change = jnp.where(lane == 0, change + half_courant * (wind_west * (tracer_west + t)), change)
         next_out[...] = (t + change).reshape(LEV, ROWS, LANES)[:, :, :COLS]
 
+        @pl.when(any_south)
+        def _():
+            next_out[:, 0, :] = next_out[:, 0, :] + from_south()[:, :COLS]
+
+        @pl.when(any_north)
+        def _():
+            next_out[:, ROWS - 1, :] = next_out[:, ROWS - 1, :] + from_north()[:, :COLS]
+
     @pl.when(is_source)
     def _():
-        t, u, change, lane = change_within()
-        increment[...] = change
-        last_wind = 0.5 * courant_number * u[:, COLS - 1 : COLS]
-        marked = jnp.where(lane == COLS, t[:, 0:1], change)
-        marked = jnp.where(lane == COLS + 1, last_wind, marked)
-        marked = jnp.where(lane == COLS + 2, last_wind * t[:, COLS - 1 : COLS], marked)
-        for level in range(LEV):
-            by_row[:, level, :] = marked[level * ROWS : (level + 1) * ROWS, :]
+        @pl.when(has_south)
+        def _():
+            take(south_in, edge_recv.at[0])
+            by_row[0] = by_row[0] + from_south()
+
+        @pl.when(has_north)
+        def _():
+            take(north_in, edge_recv.at[1])
+            by_row[ROWS - 1] = by_row[ROWS - 1] + from_north()
 
         @pl.when(low_seam)
         def _():
@@ -584,27 +594,27 @@
     @pl.when(low_seam)
     def _():
         send(
-            south_edge, seam_other.at[lon], seam_send.at[0], seam_recv.at[0], SEAM_LON, other_lat
+            south_edge, seam_other.at[lon], seam_send.at[0], seam_recv.at[0], other_seam_lon, other_lat
         ).start()
 
     @pl.when(high_seam)
     def _():
         send(
-            north_edge, seam_other.at[lon, 0], seam_send.at[0], seam_recv.at[0], SEAM_LON, other_lat
+            north_edge, seam_other.at[lon, 0], seam_send.at[0], seam_recv.at[0], other_seam_lon, other_lat
         ).start()
 
     @pl.when(jnp.logical_not(is_relay))
     def _():
         heard_along(2 * NEAR, line_sem.at[1])
 
-    @pl.when(jnp.logical_and(at_seam, lon != SEAM_LON))
+    @pl.when(jnp.logical_and(at_seam, lon != own_seam_lon))
     def _():
         send(
             seam_own.at[lon],
             seam_own.at[lon],
             seam_send.at[1],
             seam_recv.at[1],
-            SEAM_LON,
+            own_seam_lon,
             lat,
         ).start()
 
@@ -648,6 +658,12 @@
     @pl.when(half == 1)
     def _():
         each(SOURCES, lambda s: to_worker(s, 1))
+
+    @pl.when(jnp.logical_or(is_worker, seam_worker))
+    def _():
+        fh[...], fl[...] = split_value(forward[...])
+        ih[...], il[...] = split_value(inverse[...])
+        wh[...], wl[...] = split_value(within[...])
 
     @pl.when(jnp.logical_not(bridge))
     def _():
@@ -745,7 +761,11 @@
         def _():
             each(N_LON, to_own_line)
 
-        each(N_LON, lambda to: to_seam(to, other_lat, seam_back_send.at[0]))
+        def from_ends(k):
+            step = lax.div(k, 2)
+            return jnp.where(lax.rem(k, 2) == 0, step, N_LON - 1 - step)
+
+        each(N_LON, lambda k: to_seam(from_ends(k), other_lat, seam_back_send.at[0]))
 
         @pl.when(half == 1)
         def _():
@@ -764,6 +784,12 @@
         send(far_in.at[0], north_in, far_send, edge_recv.at[1], lon, opposite - 1).start()
 
     @pl.when(jnp.logical_and(is_source, jnp.logical_not(all_polar)))
+    def _():
+        plain_rows()
+
+    from_far = jnp.logical_or(far_north, far_south)
+
+    @pl.when(jnp.logical_not(jnp.logical_or(is_source, from_far)))
     def _():
         plain_rows()
 
@@ -823,6 +849,11 @@
         slot_in[half * SOURCES + s] = returned[s, half]
 
     each(SOURCES, go_home)
+
+    @pl.when(from_far)
+    def _():
+        plain_rows()
+
     take(slot_in.at[pl.ds(0, SOURCES)], cross_recv)
     for pair in range(2):
 
@@ -832,11 +863,6 @@
 
     for slot in range(SLOTS):
         slots_out[slot] = slot_in[plan[56 + slot, 0]][:, :COLS]
-
-    @pl.when(jnp.logical_not(is_source))
-    def _():
-        increment[...] = change_within()[2]
-        plain_rows()
 
     @pl.when(is_source)
     def _():

time: 65.3 us -> 71.6 us (1.096)
  the two profiles are of different devices: /device:TPU:290 before, /device:TPU:226 now
where the time goes in v7:
time: 71.6 us; the launch traced here: 71.4 us
  Pallas kernels  69.5 us (97%)
  local copies, waits for them, and re-layouts  1.31 us (2%)
    pallas_call x1, Pallas kernels, shards(): pl.pallas_call(substep_kernel, out_shape=(jax.ShapeDtypeStruct(block, f32...  69.5 us

profile of v7, /device:TPU:226, one launch (start us, length us, event | category | flops | bytes accessed | tf_op | source)
XLA Modules:
  0.0 71.4 jit_solution(9924926976288026093)
XLA Ops:
  0.6 69.5 %substep.1 = (f32[8,24,225]{2,1,0:T(8,128)S(1)}, f32[8,8,225]{2,1,0:T(8,128)S(1)}) custom-call(s32[2,128]{1,0:T(2,128)} %bitcast.2, s32[2,128]{1,0:T(2,128)} %bitcast.3, s32[8,256]{1,0:T(8,128)} %constant.17.clone.polar_hbm, f32[8,24,225]{2,1,0:T(8,128)} %tracer_hbm.1, f32[8,24,225]{2,1,0:T(8,128)} %zonal_hbm.1, f32[8,24,225]{2,1,0:T(8,128)} %merid_hbm.1, ...), custom_call_target="tpu_custom_call" | custom-call | tf_op jit(solution)/shard_map/substep/pallas_call | solution.py:963
  70.1 0.7 copy.15
  70.8 0.6 copy.16

commit v8 on v7

--- a/solution.py
+++ b/solution.py
@@ -17,7 +17,6 @@
 SOURCES, PLACES = 6, 16
 SEAM_LOW = (3, 27)
 SEAM_LON = 15
-LATE_SEAM_LON = 21
 SEAM_LINES = (3, 4, 27, 28)
 RELAYS = (10, 7, 24, 21)
 ENTRIES = 72
@@ -300,14 +299,12 @@
     work_source, work_half = lax.div(worker, 2), lax.rem(worker, 2)
     across = jnp.logical_and(is_worker, work_half != half)
     east, west = lax.rem(lon + 1, N_LON), lax.rem(lon + N_LON - 1, N_LON)
-    own_seam_lon = jnp.where(half == 0, SEAM_LON, LATE_SEAM_LON)
-    other_seam_lon = jnp.where(half == 0, LATE_SEAM_LON, SEAM_LON)
     low_seam = is_any(lat, SEAM_LOW)
     high_seam = is_any(lat, [low + 1 for low in SEAM_LOW])
     at_seam = jnp.logical_or(low_seam, high_seam)
     seam_side = jnp.where(high_seam, 1, 0)
     other_lat = jnp.where(high_seam, lat - 1, lat + 1)
-    seam_worker = jnp.logical_and(at_seam, lon == own_seam_lon)
+    seam_worker = jnp.logical_and(at_seam, lon == SEAM_LON)
     has_north, has_south = lax.rem(lat, 4) != 3, lax.rem(lat, 4) != 0
     far_north = jnp.logical_not(jnp.logical_or(has_north, jnp.logical_or(low_seam, lat == N_LAT - 1)))
     far_south = jnp.logical_not(jnp.logical_or(has_south, jnp.logical_or(high_seam, lat == 0)))
@@ -377,7 +374,7 @@
 
     @pl.when(at_seam)
     def _():
-        greet(other_seam_lon, far_relay)
+        greet(SEAM_LON, far_relay)
 
         @pl.when(seam_worker)
         def _():
@@ -463,7 +460,7 @@
 
         + jnp.where(bridge, 1, 0)
         + jnp.where(is_relay, 1, 0)
-        + jnp.where(jnp.logical_and(is_relay, lon == own_seam_lon), N_LON, 0),
+        + jnp.where(jnp.logical_and(is_relay, lon == SEAM_LON), N_LON, 0),
     )
 
     @pl.when(has_north)
@@ -594,27 +591,27 @@
     @pl.when(low_seam)
     def _():
         send(
-            south_edge, seam_other.at[lon], seam_send.at[0], seam_recv.at[0], other_seam_lon, other_lat
+            south_edge, seam_other.at[lon], seam_send.at[0], seam_recv.at[0], SEAM_LON, other_lat
         ).start()
 
     @pl.when(high_seam)
     def _():
         send(
-            north_edge, seam_other.at[lon, 0], seam_send.at[0], seam_recv.at[0], other_seam_lon, other_lat
+            north_edge, seam_other.at[lon, 0], seam_send.at[0], seam_recv.at[0], SEAM_LON, other_lat
         ).start()
 
     @pl.when(jnp.logical_not(is_relay))
     def _():
         heard_along(2 * NEAR, line_sem.at[1])
 
-    @pl.when(jnp.logical_and(at_seam, lon != own_seam_lon))
+    @pl.when(jnp.logical_and(at_seam, lon != SEAM_LON))
     def _():
         send(
             seam_own.at[lon],
             seam_own.at[lon],
             seam_send.at[1],
             seam_recv.at[1],
-            own_seam_lon,
+            SEAM_LON,
             lat,
         ).start()
 
@@ -761,11 +758,7 @@
         def _():
             each(N_LON, to_own_line)
 
-        def from_ends(k):
-            step = lax.div(k, 2)
-            return jnp.where(lax.rem(k, 2) == 0, step, N_LON - 1 - step)
-
-        each(N_LON, lambda k: to_seam(from_ends(k), other_lat, seam_back_send.at[0]))
+        each(N_LON, lambda to: to_seam(to, other_lat, seam_back_send.at[0]))
 
         @pl.when(half == 1)
         def _():

time: 71.6 us -> 65.1 us (0.909)
  the two profiles are of different devices: /device:TPU:226 before, /device:TPU:290 now
where the time goes in v8:
time: 65.1 us; the launch traced here: 65 us
  Pallas kernels  63 us (97%)
  local copies, waits for them, and re-layouts  1.31 us (2%)
    pallas_call x1, Pallas kernels, shards(): pl.pallas_call(substep_kernel, out_shape=(jax.ShapeDtypeStruct(block, f32...  63 us
    unnamed x2, local copies, waits for them, and re-layouts  1.31 us

profile of v8, /device:TPU:290, one launch (start us, length us, event | category | flops | bytes accessed | tf_op | source)
XLA Modules:
  0.0 65.0 jit_solution(6715948104377971881)
XLA Ops:
  0.6 63.0 %substep.1 = (f32[8,24,225]{2,1,0:T(8,128)S(1)}, f32[8,8,225]{2,1,0:T(8,128)S(1)}) custom-call(s32[2,128]{1,0:T(2,128)} %bitcast.2, s32[2,128]{1,0:T(2,128)} %bitcast.3, s32[8,256]{1,0:T(8,128)} %constant.17.clone.polar_hbm, f32[8,24,225]{2,1,0:T(8,128)} %tracer_hbm.1, f32[8,24,225]{2,1,0:T(8,128)} %zonal_hbm.1, f32[8,24,225]{2,1,0:T(8,128)} %merid_hbm.1, ...), custom_call_target="tpu_custom_call" | custom-call | tf_op jit(solution)/shard_map/substep/pallas_call | solution.py:956
  63.7 0.7 %copy.15 = f32[8,24,225]{2,1,0:T(8,128)} copy(f32[8,24,225]{2,1,0:T(8,128)S(1)} %get-tuple-element.4) | data formatting | bytes 345600
  64.3 0.6 copy.16
